TPU v7x, 256 devices: a whole 4x4x8 slice. The times are simulated.
256 devices in a mesh: seq: 16 (over x_lo, z), tp: 16 (over y, x_hi, core).
Axes of the slice: x: 4 (x_hi: 2, x_lo: 2; x = x_hi * 2 + x_lo), y: 4, z: 8, core: 2. Of those that a mesh axis runs over, the one named last changes fastest.
Arguments:
- inputs: bfloat16 [32768, 1536], P('seq', 'tp'), may hold values from -6 to 6
- grad_out: bfloat16 [32768, 1536], P('seq', 'tp'), may hold values from -6 to 6
- kernel: float32 [15, 1536], P(None, 'tp'), may hold values from -2 to 2
- ln_gain: float32 [1536], replicated, may hold values from 0.4 to 2.5
- layer_scale: float32 [1536], replicated, may hold values from 0.2 to 2
- w_up: bfloat16 [1536, 6144], P(None, 'tp'), may hold values from -0.15625 to 0.15625
- w_down: bfloat16 [6144, 1536], P('tp'), may hold values from -0.078125 to 0.078125
Outputs:
- grad_inputs: bfloat16 [32768, 1536], P('seq', 'tp')
- grad_up: float32 [1536, 6144], P('seq', 'tp')
- grad_down_t: float32 [1536, 6144], P('seq', 'tp')
- grad_kernel: float32 [15, 1536], P(None, 'tp')
All inputs are finite; a program needn't handle non-finite values.
Results may differ from a plain program's by a relative error of at most 0.023.
Values may be sent and summed in bfloat16 or wider, within the bound.
A program may use at most 128 MiB of HBM per device.

v0:
```python
import math

import jax
import jax.numpy as jnp
from jax import lax
from jax.sharding import PartitionSpec as P


def extended(cells, sides, width):
    for axis, dim in sides:
        count = lax.axis_size(axis)
        ends = count - 1
        head = lax.slice_in_dim(cells, 0, width, axis=dim)
        tail = lax.slice_in_dim(cells, cells.shape[dim] - width, cells.shape[dim], axis=dim)
        cells = jnp.concatenate(
            [
                lax.ppermute(tail, axis, [(i, (i + 1) % count) for i in range(ends)]),
                cells,
                lax.ppermute(head, axis, [((i + 1) % count, i) for i in range(ends)]),
            ],
            axis=dim,
        )
    return cells


def gelu_value(pre):
    return 0.5 * pre * (1.0 + lax.erf(pre * 0.7071067811865476))


def gelu_slope(pre):
    return (
        0.5 * (1.0 + lax.erf(pre * 0.7071067811865476))
        + pre * jnp.exp(-0.5 * pre * pre) * 0.3989422804014327
    )


def contract_first(left, right):
    return lax.dot_general(
        left, right, (((0,), (0,)), ((), ())), preferred_element_type=jnp.float32
    )


def contract_last(left, right):
    return lax.dot_general(
        left, right, (((1,), (1,)), ((), ())), preferred_element_type=jnp.float32
    )


def local(inputs, grad_out, kernel, ln_gain, layer_scale, w_up, w_down):
    positions, local_width = inputs.shape
    groups = lax.axis_size("tp")
    channels = local_width * groups
    unit_width = w_up.shape[1]
    kernel_len = kernel.shape[0]
    reach = kernel_len // 2
    total = positions * lax.axis_size("seq")
    col_start = lax.axis_index("tp") * local_width
    gain_local = lax.dynamic_slice_in_dim(ln_gain, col_start, local_width, 0)
    padded = extended(inputs, (("seq", 0),), reach).astype(jnp.float32)
    conv = sum(
        (kernel[offset] * padded[offset : offset + positions] for offset in range(kernel_len))
    )
    row_sum, row_sq = lax.psum((jnp.sum(conv, axis=1), jnp.sum(conv * conv, axis=1)), "tp")
    row_mean = (row_sum / channels)[:, None]
    row_var = (row_sq / channels)[:, None] - row_mean * row_mean
    rstd = lax.rsqrt(row_var + 1e-06)
    nhat = (conv - row_mean) * rstd
    normed = (nhat * gain_local).astype(jnp.bfloat16)
    normed_all, grad_all = (
        lax.all_gather(normed, "tp", axis=1, tiled=True),
        lax.all_gather(grad_out, "tp", axis=1, tiled=True),
    )
    scaled = (layer_scale * grad_all.astype(jnp.float32)).astype(jnp.bfloat16)
    pre_act = jnp.dot(normed_all, w_up, preferred_element_type=jnp.float32)
    hidden = gelu_value(pre_act).astype(jnp.bfloat16)
    grad_hidden = contract_last(scaled, w_down)
    grad_pre = (grad_hidden * gelu_slope(pre_act)).astype(jnp.bfloat16)
    grad_normed = (
        lax.psum_scatter(
            contract_last(w_up, grad_pre).astype(jnp.bfloat16),
            "tp",
            scatter_dimension=0,
            tiled=True,
        )
        .astype(jnp.float32)
        .T
    )
    scaled_g = grad_normed * gain_local
    first_sum, second_sum = lax.psum(
        (jnp.sum(scaled_g, axis=1), jnp.sum(scaled_g * nhat, axis=1)), "tp"
    )
    grad_conv = rstd * (
        scaled_g - (first_sum / channels)[:, None] - nhat * (second_sum / channels)[:, None]
    )
    grad_pad = extended(grad_conv.astype(jnp.bfloat16), (("seq", 0),), reach).astype(
        grad_conv.dtype
    )
    grad_inputs = grad_out.astype(jnp.float32) + sum(
        (
            kernel[offset] * grad_pad[2 * reach - offset : 2 * reach - offset + positions]
            for offset in range(kernel_len)
        )
    )
    factor = 1.0 / math.sqrt(total)
    tap_local = jnp.stack(
        [
            jnp.sum(grad_conv * padded[offset : offset + positions], axis=0)
            for offset in range(kernel_len)
        ]
    )
    grad_kernel = lax.psum(tap_local, "seq") * factor
    both_grads = (
        lax.psum_scatter(
            jnp.concatenate(
                [contract_first(normed_all, grad_pre), contract_first(scaled, hidden)], axis=1
            ).astype(jnp.bfloat16),
            "seq",
            scatter_dimension=0,
            tiled=True,
        ).astype(jnp.float32)
        * factor
    )
    return (
        grad_inputs.astype(jnp.bfloat16),
        both_grads[:, :unit_width],
        both_grads[:, unit_width:],
        grad_kernel,
    )


def solution(mesh):
    in_specs = (
        P("seq", "tp"),
        P("seq", "tp"),
        P(None, "tp"),
        P(),
        P(),
        P(None, "tp"),
        P("tp", None),
    )
    out_specs = (P("seq", "tp"), P("seq", "tp"), P("seq", "tp"), P(None, "tp"))
    return jax.shard_map(local, mesh=mesh, in_specs=in_specs, out_specs=out_specs, check_vma=False)
```

profile of v0, /device:TPU:2, one launch (start us, length us, event | category | flops | bytes accessed | tf_op | source)
XLA Modules:
  0.0 548.5 jit_solution(8953664723763102027)
XLA Ops:
  7.2 0.9 fusion.32
  8.1 7.7 %collective-permute-start.1 = (bf16[7,96]{0,1:T(8,128)(2,1)S(1)}, bf16[7,96]{0,1:T(8,128)(2,1)S(1)}, u32[]{:S(2)}, u32[]{:S(2)}) collective-permute-start(bf16[7,96]{0,1:T(8,128)(2,1)S(1)} %get-tuple-element.39), channel_id=1, source_target_pairs={{16,0},{32,16},{48,32},{64,48},{80,64},{96,80},{112,96},{128,112},... | collective-permute-start | bytes 4040 | tf_op jit(solution)/shard_map/ppermute | solution.py:19
  15.9 1.9 collective-permute-start
  17.8 1.0 slice_bitcast_fusion.14
  19.6 4.1 collective-permute-done
  23.7 1.4 concatenate.10
  25.2 3.5 multiply_reduce_fusion.15
  28.7 67.7 %all-reduce.1 = (f32[2048]{0:T(1024)S(1)}, f32[2048]{0:T(1024)S(1)}) all-reduce(f32[2048]{0:T(1024)S(1)} %get-tuple-element.28, f32[2048]{0:T(1024)S(1)} %get-tuple-element.27), channel_id=1, replica_groups=mesh['seq'=16,'tp'=16] {'tp'}, use_global_device_ids=true, to_apply=%region_3.0 | all-reduce | flops 4096 | bytes 32768 | tf_op jit(solution)/shard_map/psum | solution.py:63
  96.4 0.9 multiply_convert_fusion.5
  98.2 59.6 %all-gather.5.cloned.1.call-done = bf16[2048,1536]{0,1:T(8,128)(2,1)} async-done(((bf16[2048,96]{0,1:T(8,128)(2,1)}), bf16[2048,1536]{0,1:T(8,128)(2,1)}) %all-gather.5.cloned.1.call-update) | async-done | bytes 6291472 | tf_op jit(solution)/shard_map/all_gather | solution.py:70
  157.8 7.9 %fusion.33 = f32[2048,384]{1,0:T(8,128)} fusion(bf16[2048,1536]{0,1:T(8,128)(2,1)} %all-gather.5.cloned.1.call-done, bf16[1536,384]{1,0:T(8,128)(2,1)S(1)} %copy-done), kind=kOutput, calls=%fused_computation.98 | convolution fusion | flops 2415919104 | bytes 10616832 | tf_op jit(solution)/shard_map/dot_general | solution.py:74
  165.7 61.9 %all-gather.3.cloned.1.call-done = bf16[2048,1536]{0,1:T(8,128)(2,1)} async-done(((bf16[2048,96]{0,1:T(8,128)(2,1)}), bf16[2048,1536]{0,1:T(8,128)(2,1)}) %all-gather.3.cloned.1.call-update) | async-done | bytes 6291472 | tf_op jit(solution)/shard_map/all_gather | solution.py:71
  227.6 6.7 %convolution_convert_fusion.1 = bf16[1536,384]{0,1:T(8,128)(2,1)S(1)} fusion(bf16[2048,1536]{0,1:T(8,128)(2,1)} %all-gather.3.cloned.1.call-done, f32[1536]{0:T(1024)S(1)} %copy-done.3, f32[2048,384]{1,0:T(8,128)} %fusion.33), kind=kOutput, calls=%fused_computation.12 | convolution fusion | flops 2429878272 | bytes 10622976 | tf_op jit(solution)/shard_map/dot_general | solution.py:38
  234.4 4.8 fusion.6
  239.2 2.9 convolution_convert_fusion.2
  242.1 1.6 pad_maximum_fusion
  243.7 4.3 copy.23
  248.0 6.9 %fusion = bf16[1536,2048]{0,1:T(8,128)(2,1)} fusion(bf16[2048,384]{1,0:T(8,128)(2,1)} %copy-done.4, bf16[1536,384]{1,0:T(8,128)(2,1)S(1)} %copy-done), kind=kOutput, calls=%fused_computation.2 | convolution fusion | flops 2419064832 | bytes 9043968 | tf_op jit(solution)/shard_map/dot_general | solution.py:44
  254.9 8.6 %copy.21 = bf16[1536,2048]{1,0:T(8,128)(2,1)} copy(bf16[1536,2048]{0,1:T(8,128)(2,1)} %fusion) | data formatting | bytes 12582912
  263.6 57.4 %reduce-scatter.9.cloned.1.call-done = bf16[96,768]{1,0:T(8,128)(2,1)} async-done(((bf16[1536,768]{1,0:T(8,128)(2,1)}), bf16[96,768]{1,0:T(8,128)(2,1)}) %reduce-scatter.9.cloned.1.call-update) | async-done | bytes 147472
  321.0 1.1 copy.24
  322.2 0.8 copy.20
  323.7 95.0 %reduce-scatter.7.cloned.1.call-done = bf16[96,2048]{1,0:T(8,128)(2,1)} async-done(((bf16[1536,2048]{1,0:T(8,128)(2,1)}), bf16[96,2048]{1,0:T(8,128)(2,1)}) %reduce-scatter.7.cloned.1.call-update) | async-done | bytes 393232 | tf_op jit(solution)/shard_map/reduce_scatter | solution.py:79
  418.7 1.1 fusion.27
  419.9 1.2 fusion.26
  421.1 66.0 %all-reduce = (f32[2048]{0:T(1024)S(1)}, f32[2048]{0:T(1024)S(1)}) all-reduce(f32[2048]{0:T(1024)S(1)} %fusion.26, f32[2048]{0:T(1024)S(1)} %fusion.27), channel_id=1, replica_groups=mesh['seq'=16,'tp'=16] {'tp'}, use_global_device_ids=true, to_apply=%region_8.0 | all-reduce | flops 4096 | bytes 32768 | tf_op jit(solution)/shard_map/psum | solution.py:89
  487.1 5.0 multiply_reduce_fusion
  492.2 34.5 %psum.39 = f32[15,96]{1,0:T(8,128)S(1)} all-reduce(f32[15,96]{1,0:T(8,128)S(1)} %stack.63), channel_id=1, replica_groups=mesh['seq'=16,'tp'=16] {'seq'}, use_global_device_ids=true, to_apply=%region_25.0 | all-reduce | flops 1440 | bytes 11520 | tf_op jit(solution)/shard_map/psum | solution.py:111
  526.7 1.9 collective-permute-start.3
  528.6 3.9 collective-permute-start.2
  533.2 3.3 collective-permute-done.2
  536.9 5.1 fusion.10
  (39 shorter events, 4.0 us)
Async XLA Ops:
  7.2 150.6 %copy-start = (bf16[1536,384]{1,0:T(8,128)(2,1)S(1)}, bf16[1536,384]{1,0:T(8,128)(2,1)}, u32[]{:S(2)}) copy-start(bf16[1536,384]{1,0:T(8,128)(2,1)} %param.12) | copy-start | bytes 3538948
  7.2 150.6 %all-gather.5.cloned.1.call-start = ((), (), s32[]{:S(2)}) async-start(), calls=%async_computation.3 | async-start | bytes 6684672 | tf_op jit(solution)/shard_map/all_gather | solution.py:70
  8.1 11.4 %collective-permute-start.1 = (bf16[7,96]{0,1:T(8,128)(2,1)S(1)}, bf16[7,96]{0,1:T(8,128)(2,1)S(1)}, u32[]{:S(2)}, u32[]{:S(2)}) collective-permute-start(bf16[7,96]{0,1:T(8,128)(2,1)S(1)} %get-tuple-element.39), channel_id=1, source_target_pairs={{16,0},{32,16},{48,32},{64,48},{80,64},{96,80},{112,96},{128,112},... | collective-permute-start | bytes 4040 | tf_op jit(solution)/shard_map/ppermute | solution.py:19
  15.9 7.8 %collective-permute-start = (bf16[7,96]{0,1:T(8,128)(2,1)S(1)}, bf16[7,96]{0,1:T(8,128)(2,1)S(1)}, u32[]{:S(2)}, u32[]{:S(2)}) collective-permute-start(bf16[7,96]{0,1:T(8,128)(2,1)S(1)} %get-tuple-element.40), channel_id=1, source_target_pairs={{0,16},{16,32},{32,48},{48,64},{64,80},{80,96},{96,112},{112,128},... | collective-permute-start | bytes 4040 | tf_op jit(solution)/shard_map/ppermute | solution.py:17
  97.3 130.3 %all-gather.3.cloned.1.call-start = ((), (), s32[]{:S(2)}) async-start(), calls=%async_computation.2 | async-start | bytes 6684672 | tf_op jit(solution)/shard_map/all_gather | solution.py:71
  98.0 129.6 %copy-start.3 = (f32[1536]{0:T(1024)S(1)}, f32[1536]{0:T(1024)}, u32[]{:S(2)}) copy-start(f32[1536]{0:T(1024)} %param.11) | copy-start | bytes 18436
  98.0 223.0 %reduce-scatter.9.cloned.1.call-start = ((), (), s32[]{:S(2)}) async-start(), calls=%async_computation.5 | async-start | bytes 2506752
  227.6 6.7 %copy-start.1 = (bf16[2048,1536]{0,1:T(8,128)(2,1)S(1)}, bf16[2048,1536]{0,1:T(8,128)(2,1)}, u32[]{:S(2)}) copy-start(bf16[2048,1536]{0,1:T(8,128)(2,1)} %all-gather.3.cloned.1.call-done) | copy-start | bytes 18874372
  227.6 6.7 %copy-start.2 = (bf16[384,1536]{1,0:T(8,128)(2,1)S(1)}, bf16[384,1536]{1,0:T(8,128)(2,1)}, u32[]{:S(2)}) copy-start(bf16[384,1536]{1,0:T(8,128)(2,1)} %param.13) | copy-start | bytes 3538948
  227.6 6.8 %copy-start.5 = (f32[2048,384]{1,0:T(8,128)S(1)}, f32[2048,384]{1,0:T(8,128)}, u32[]{:S(2)}) copy-start(f32[2048,384]{1,0:T(8,128)} %fusion.33) | copy-start | bytes 9437188
  227.6 11.6 %slice-start = ((s8[6291456]{0:T(1024)(128)(4,1)}), s8[4194304]{0:T(1024)(128)(4,1)S(1)}, s32[]{:S(2)}) async-start(s8[6291456]{0:T(1024)(128)(4,1)} %bitcast.81), calls=%async_computation.6 | async-start | bytes 8388608
  234.4 4.8 slice-start.1
  239.2 2.9 copy-start.4
  248.0 170.7 %reduce-scatter.7.cloned.1.call-start = ((), (), s32[]{:S(2)}) async-start(), calls=%async_computation.4 | async-start | bytes 6684672 | tf_op jit(solution)/shard_map/reduce_scatter | solution.py:79
  526.7 6.5 %collective-permute-start.3 = (bf16[7,96]{0,1:T(8,128)(2,1)S(1)}, bf16[7,96]{0,1:T(8,128)(2,1)S(1)}, u32[]{:S(2)}, u32[]{:S(2)}) collective-permute-start(bf16[7,96]{0,1:T(8,128)(2,1)S(1)} %get-tuple-element.37), channel_id=1, source_target_pairs={{16,0},{32,16},{48,32},{64,48},{80,64},{96,80},{112,96},{128,112},... | collective-permute-start | bytes 4040 | tf_op jit(solution)/shard_map/ppermute | solution.py:19
  528.6 7.8 %collective-permute-start.2 = (bf16[7,96]{0,1:T(8,128)(2,1)S(1)}, bf16[7,96]{0,1:T(8,128)(2,1)S(1)}, u32[]{:S(2)}, u32[]{:S(2)}) collective-permute-start(bf16[7,96]{0,1:T(8,128)(2,1)S(1)} %get-tuple-element.38), channel_id=1, source_target_pairs={{0,16},{16,32},{32,48},{48,64},{64,80},{80,96},{96,112},{112,128},... | collective-permute-start | bytes 4040 | tf_op jit(solution)/shard_map/ppermute | solution.py:17
Sparse Core Ops, SparseCore 0:
  97.4 60.3 all-gather.4
  160.6 66.9 all-gather.2
  248.1 72.8 reduce-scatter.8
  325.3 93.3 reduce-scatter.6
where the time goes:
time: 549 us
  waiting for transfers between devices  282 us (51%)
  blocking collectives  168 us (31%)
  matrix products  29.2 us (5%)
  local copies, waits for them, and re-layouts  20.2 us (4%)
  other arithmetic  19.1 us (3%)
  starting transfers between devices  15.8 us (3%)
  between operations  14 us (3%)
    reduce_scatter x1, waiting for transfers between devices, local(): lax.psum_scatter(contract_last(w_up, grad_pre).astype(jnp.bfloat16), 'tp'...  95 us
    psum x1, blocking collectives, local(): lax.psum((jnp.sum(conv, axis=1), jnp.sum(conv * conv, axis=1)), 'tp')  67.7 us
    psum x1, blocking collectives, local(): lax.psum((jnp.sum(scaled_g, axis=1), jnp.sum(scaled_g * nhat, axis=1)), '...  66 us
    all_gather x1, waiting for transfers between devices, local(): lax.all_gather(grad_out, 'tp', axis=1, tiled=True)  61.9 us
    all_gather x1, waiting for transfers between devices, local(): lax.all_gather(normed, 'tp', axis=1, tiled=True)  59.6 us
    unnamed x5, waiting for transfers between devices  58.2 us
    psum x1, blocking collectives, local(): grad_kernel = lax.psum(tap_local, 'seq') * factor  34.5 us
    unnamed x21, local copies, waits for them, and re-layouts  15.6 us
  transfers between devices with their start and end apart: 8, of which 6 were waited for; matrix products, arithmetic and copies ran while one was open for 5% of the time, Pallas kernels for 0%

commit v1 on v0

v1 whole, which is shorter than its diff:
```python
import functools
import math

import jax
import jax.numpy as jnp
from jax import lax
from jax.experimental import pallas as pl
from jax.experimental.pallas import tpu as pltpu
from jax.sharding import PartitionSpec as P

MESH = pl.DeviceIdType.MESH
BF = jnp.bfloat16
F32 = jnp.float32

TP = 16
NY = 4
SEQ = 16
NZ = 8
W = 96
D = 1536
TOK = 2048
HALF = TOK // 2
NC = 4
TC = HALF // NC
U = 384
KW = 15
REACH = KW // 2
PAD = 128


def nn(a, b):
    return jnp.dot(a, b, preferred_element_type=F32)


def nt(a, b):
    return lax.dot_general(a, b, (((1,), (1,)), ((), ())), preferred_element_type=F32)


def shifted(x, by):
    width = x.shape[1]
    return pltpu.roll(x, (-by) % width, 1) if by else x


def body(
    x_t, go_t, taps, gain_l, scale_l, gain_all, wu, wu_t, wd,
    gi_t, gu, gd, gk,
    s_st, n_st, g_s, g_n, xp, cv, hin, st_s, st_r, mr, wu_p, wu_tp, wd_p, pre_s, gh_s,
    hid, gpr, pf, s1, r1, s2, r2, s3, r3, own, bst, bst_r, gc, gch_s, gch, gkp, gks, gkr,
    wf, c_s, c_r, z_s, z_r, x_s, x_r,
    halo_ss, halo_rs, w_ss, w_rs, st_ss, st_rs, a1_ss, a1_rs, a2_ss, a2_rs, a3_ss, a3_rs,
    r1_ss, r1_rs, r2_ss, r2_rs, r3_ss, r3_rs, b_ss, b_rs, gh_ss, gh_rs, gk_ss, gk_rs,
    c_ss, c_rs, z_ss, z_rs, x_ss, x_rs,
):
    tp = lax.axis_index("tp")
    sq = lax.axis_index("seq")
    k = lax.rem(tp, 2)
    xh = lax.rem(tp // 2, 2)
    y = tp // 4
    xl = sq // NZ
    z = lax.rem(sq, NZ)

    def at(y_, xh_, k_):
        return {"seq": sq, "tp": (y_ * 2 + xh_) * 2 + k_}

    def send(src, dst, ss, rs, dev):
        return pltpu.make_async_remote_copy(
            src_ref=src, dst_ref=dst, send_sem=ss, recv_sem=rs, device_id=dev, device_id_type=MESH
        )

    up, down = lax.rem(y + 1, NY), lax.rem(y + NY - 1, NY)
    anti = lax.rem(y + 2, NY)
    y_dev = (at(up, xh, k), at(down, xh, k))
    other = 1 - k
    near = (at(y, 1 - xh, k), at(y, xh, other), at(y, 1 - xh, other))
    sq_next, sq_prev = lax.rem(sq + 1, SEQ), lax.rem(sq + SEQ - 1, SEQ)
    sq_dev = ({"seq": sq_next, "tp": tp}, {"seq": sq_prev, "tp": tp})
    z_dev = (
        {"seq": xl * NZ + lax.rem(z + 1, NZ), "tp": tp},
        {"seq": xl * NZ + lax.rem(z + NZ - 1, NZ), "tp": tp},
    )
    x_dev = {"seq": (1 - xl) * NZ + z, "tp": tp}
    my_rows = pl.ds(pl.multiple_of(tp * W, 32), W)

    def y_rows(which, first=0, count=4 * W):
        return pl.ds(pl.multiple_of(which * (4 * W) + first, 32), count)

    barrier = pltpu.get_barrier_semaphore()
    for j in range(1, TP):
        pl.semaphore_signal(
            barrier, inc=1, device_id={"seq": sq, "tp": lax.rem(tp + j, TP)}, device_id_type=MESH
        )
    for j in range(1, SEQ):
        pl.semaphore_signal(
            barrier, inc=1, device_id={"seq": lax.rem(sq + j, SEQ), "tp": tp}, device_id_type=MESH
        )
    pl.semaphore_wait(barrier, TP + SEQ - 2)

    def halo(d):
        src = x_t.at[:, pl.ds(TOK - PAD, PAD)] if d == 0 else x_t.at[:, pl.ds(0, PAD)]
        return send(src, hin.at[d], halo_ss.at[d], halo_rs.at[d], sq_dev[d])

    def weight(i):
        src, dst = ((wd, wd_p), (wu_t, wu_tp), (wu, wu_p))[i]
        return send(src, dst, w_ss.at[i], w_rs.at[i], near[1])

    def stat_out(j):
        return send(
            st_s, st_r.at[tp], st_ss.at[j], st_rs.at[tp], {"seq": sq, "tp": lax.rem(tp + j, TP)}
        )

    def stat_in(j):
        src = lax.rem(tp + j, TP)
        return send(st_s, st_r.at[src], st_ss.at[j], st_rs.at[src], {"seq": sq, "tp": src})

    staged, full = (s_st, n_st), (g_s, g_n)

    def ag1(a, c, j):
        src = staged[a].at[k if j == 0 else other, c]
        i = (a * NC + c) * 3 + j
        return send(src, full[a].at[c, my_rows], a1_ss.at[i], a1_rs.at[i], near[j])

    def ag2(a, c, d):
        part = full[a].at[c, y_rows(y)]
        i = (a * NC + c) * 2 + d
        return send(part, part, a2_ss.at[i], a2_rs.at[i], y_dev[d])

    def ag3(a, c, d):
        part = full[a].at[c, y_rows(down, 0, 2 * W) if d == 0 else y_rows(up, 2 * W, 2 * W)]
        i = (a * NC + c) * 2 + d
        return send(part, part, a3_ss.at[i], a3_rs.at[i], y_dev[d])

    def rs1(c, d):
        i = c * 2 + d
        return send(s1.at[d, c], r1.at[d, c], r1_ss.at[i], r1_rs.at[i], y_dev[d])

    def rs2(c, d):
        i = c * 2 + d
        return send(s2.at[d, c], r2.at[d, c], r2_ss.at[i], r2_rs.at[i], y_dev[d])

    def rs3(c, j):
        i = c * 3 + j
        return send(s3.at[c, j], r3.at[c, j], r3_ss.at[i], r3_rs.at[i], near[j])

    def bstat_out(j):
        return send(
            bst, bst_r.at[tp], b_ss.at[j], b_rs.at[tp], {"seq": sq, "tp": lax.rem(tp + j, TP)}
        )

    def bstat_in(j):
        src = lax.rem(tp + j, TP)
        return send(bst, bst_r.at[src], b_ss.at[j], b_rs.at[src], {"seq": sq, "tp": src})

    def ghalo(d):
        return send(gch_s.at[d], gch.at[d], gh_ss.at[d], gh_rs.at[d], sq_dev[d])

    def gk_out(j):
        return send(
            gks, gkr.at[sq], gk_ss.at[j], gk_rs.at[sq], {"seq": lax.rem(sq + j, SEQ), "tp": tp}
        )

    def gk_in(j):
        src = lax.rem(sq + j, SEQ)
        return send(gks, gkr.at[src], gk_ss.at[j], gk_rs.at[src], {"seq": src, "tp": tp})

    def core_w(i):
        return send(c_s.at[i], c_r.at[i], c_ss.at[i], c_rs.at[i], near[1])

    def ring(d, step, e):
        i = (d * 4 + step) * 2 + e
        if step == 0:
            return send(
                z_s.at[d, step, e, pl.ds(d, 1)], z_r.at[d, step, e, pl.ds(d, 1)],
                z_ss.at[i], z_rs.at[i], z_dev[d],
            )
        return send(z_s.at[d, step, e], z_r.at[d, step, e], z_ss.at[i], z_rs.at[i], z_dev[d])

    def x_swap():
        return send(x_s, x_r, x_ss.at[0], x_rs.at[0], x_dev)

    for d in range(2):
        halo(d).start()
    for c in range(NC):
        for h in range(2):
            cols = pl.ds(h * HALF + c * TC, TC)
            s_st[h, c] = (scale_l[...] * go_t[:, cols].astype(F32)).astype(BF)
        for j in (2, 0, 1):
            ag1(0, c, j).start()
        g_s[c, my_rows] = s_st[k, c]
    for i in range(3):
        weight(i).start()

    xp[:, pl.ds(PAD, TOK)] = x_t[...].astype(F32)
    for d in range(2):
        halo(d).wait_recv()
    xp[:, pl.ds(0, PAD)] = jnp.where(sq == 0, 0.0, hin[0].astype(F32))
    xp[:, pl.ds(PAD + TOK, PAD)] = jnp.where(sq == SEQ - 1, 0.0, hin[1].astype(F32))

    def conv_rows(i, sums):
        rows = pl.ds(pl.multiple_of(i * 8, 8), 8)
        x = xp[rows, :]
        t = taps[rows, :]
        total = None
        for tap in range(KW):
            term = t[:, tap : tap + 1] * shifted(x, tap - REACH)[:, PAD : PAD + TOK]
            total = term if total is None else total + term
        cv[rows, :] = total
        return sums[0] + total, sums[1] + total * total

    zero = jnp.zeros((8, TOK), F32)
    first, second = lax.fori_loop(0, W // 8, conv_rows, (zero, zero))
    st_s[0:1, :] = jnp.sum(first, axis=0, keepdims=True)
    st_s[1:2, :] = jnp.sum(second, axis=0, keepdims=True)
    for j in range(1, TP):
        stat_out(j).start()
    st_r[tp] = st_s[...]

    def pass_on_1(a, c):
        for j in range(3):
            ag1(a, c, j).wait_recv()
        for d in range(2):
            ag2(a, c, d).start()

    def pass_on_2(a, c):
        for d in range(2):
            ag2(a, c, d).wait_recv()
            ag3(a, c, d).start()

    pass_on_1(0, 0)
    for j in range(1, TP):
        stat_in(j).wait_recv()
    totals = st_r[0]
    for j in range(1, TP):
        totals = totals + st_r[j]
    mean = totals[0:1] / D
    var = totals[1:2] / D - mean * mean
    mr[0:1, :] = mean
    mr[1:2, :] = lax.rsqrt(var + 1e-06)
    for c in range(NC):
        for h in range(2):
            cols = pl.ds(h * HALF + c * TC, TC)
            nhat = (cv[:, cols] - mr[0:1, cols]) * mr[1:2, cols]
            n_st[h, c] = (nhat * gain_l[...]).astype(BF)
        for j in (2, 0, 1):
            ag1(1, c, j).start()
        g_n[c, my_rows] = n_st[k, c]

    for c in range(1, NC):
        pass_on_1(0, c)
    for c in range(NC):
        pass_on_2(0, c)
        pass_on_1(1, c)
    for i in range(3):
        weight(i).wait_recv()
    pass_on_2(1, 0)

    def rs2_step(c):
        for d, to in ((0, up), (1, down)):
            rs1(c, d).wait_recv()
            a, b = d * 2 * W, (1 - d) * 2 * W
            got = pf[c, y_rows(to, a, 2 * W)] + r1[d, c].astype(F32)
            s2[d, c, pl.ds(a, 2 * W)] = got.astype(BF)
            s2[d, c, pl.ds(b, 2 * W)] = pf[c, y_rows(to, b, 2 * W)].astype(BF)
            rs2(c, d).start()

    def rs3_step(c):
        for d in range(2):
            rs2(c, d).wait_recv()

        def group(g):
            rows = pl.ds(pl.multiple_of(g * W, 32), W)
            mine = pf[c, y_rows(y, g * W, W)]
            return mine + r2[0, c, rows].astype(F32) + r2[1, c, rows].astype(F32)

        for j, (xh_, k_) in ((2, (1 - xh, other)), (0, (1 - xh, k)), (1, (xh, other))):
            s3[c, j] = group(xh_ * 2 + k_).astype(BF)
            rs3(c, j).start()
        own[c] = group(xh * 2 + k)

    def chunk(c, carry):
        for a in range(2):
            for d in range(2):
                ag3(a, c, d).wait_recv()

        acc = jnp.zeros((8, TC), F32)
        for u, (w_t, w_d) in enumerate(((wu_t, wd), (wu_tp, wd_p))):
            pre_s[...] = nn(w_t[...], g_n[c])
            gh_s[...] = nn(w_d[...], g_s[c])

            def act(i, acc, u=u):
                rows = pl.ds(pl.multiple_of(i * 32, 32), 32)
                v = pre_s[rows, :]
                phi = 0.5 + 0.5 * lax.erf(v * 0.7071067811865476)
                slope = phi + v * jnp.exp(-0.5 * v * v) * 0.3989422804014327
                gp = (gh_s[rows, :] * slope).astype(BF)
                to = pl.ds(pl.multiple_of(u * U + i * 32, 32), 32)
                hid[c, to] = (v * phi).astype(BF)
                gpr[c, to] = gp
                return acc + jnp.sum((gp.astype(F32) * v).reshape(4, 8, TC), axis=0)

            acc = lax.fori_loop(0, U // 32, act, acc)
        second = jnp.sum(acc, axis=0, keepdims=True)

        @pl.when(c < NC - 1)
        def _():
            pass_on_2(1, c + 1)

        acc = jnp.zeros((8, TC), F32)
        for r in range(NY):
            rows = pl.ds(r * 4 * W, 4 * W)
            p = nn(wu[rows, :], gpr[c, pl.ds(0, U)]) + nn(wu_p[rows, :], gpr[c, pl.ds(U, U)])
            pf[c, rows] = p
            acc = acc + jnp.sum((gain_all[rows, :] * p).reshape(4 * W // 8, 8, TC), axis=0)
        cols = pl.ds(pl.multiple_of(c * TC, TC), TC)
        bst[0:1, cols] = jnp.sum(acc, axis=0, keepdims=True)
        bst[1:2, cols] = second
        for d in range(2):
            s1[d, c] = pf[c, y_rows(anti, d * 2 * W, 2 * W)].astype(BF)
            rs1(c, d).start()

        @pl.when(c >= 1)
        def _():
            rs2_step(c - 1)

        @pl.when(c >= 2)
        def _():
            rs3_step(c - 2)

        return carry

    lax.fori_loop(0, NC, chunk, 0)
    for j in range(1, TP):
        bstat_out(j).start()
    bst_r[tp] = bst[...]

    order = (4, 3, 5, 2, 6, 1, 7, 0)

    def block_of(off):
        return lax.rem(z + off, NZ)

    def weight_block(i, carry):
        half = (i + 1) // 2
        off = jnp.where(lax.rem(i, 2) == 1, 4 - half, 4 + half)
        off = lax.rem(off, NZ)
        b = lax.rem(z + off, NZ)
        for e in range(2):
            rows = pl.ds(pl.multiple_of(e * (NZ * W) + b * W, 32), W)
            for a, (left, right) in enumerate(((g_n, gpr), (g_s, hid))):
                total = nt(left[0, rows], right[0])
                for c in range(1, NC):
                    total = total + nt(left[c, rows], right[c])
                wf[b, e, a] = total[:, :U]
                c_s[i, e, a] = total[:, U:].astype(BF)
        core_w(i).start()
        return carry

    def ring_step(i):
        off = order[i]
        b = block_of(off)
        core_w(i).wait_recv()
        if off == 4:
            for e in range(2):
                for d in range(2):
                    got = wf[b, e, d] + c_r[i, e, d].astype(F32)
                    z_s[d, 0, e, d] = got.astype(BF)
                    ring(d, 0, e).start()
        elif off != 0:
            d = 0 if off < 4 else 1
            step = 4 - off if off < 4 else off - 4
            for e in range(2):
                ring(d, step - 1, e).wait_recv()
                for a in range(2):
                    got = wf[b, e, a] + c_r[i, e, a].astype(F32)
                    if step > 1 or a == d:
                        got = got + z_r[d, step - 1, e, a].astype(F32)
                    z_s[d, step, e, a] = got.astype(BF)
                ring(d, step, e).start()
        else:
            for e in range(2):
                for d in range(2):
                    ring(d, 3, e).wait_recv()

            def part(e, a):
                got = wf[b, e, a] + c_r[i, e, a].astype(F32)
                return got + z_r[0, 3, e, a].astype(F32) + z_r[1, 3, e, a].astype(F32)

            for a in range(2):
                x_s[a] = part(1 - xl, a).astype(BF)
            x_swap().start()
            for a in range(2):
                wf[b, xl, a] = part(xl, a)

    lax.fori_loop(0, 3, weight_block, 0)
    rs2_step(NC - 1)
    rs3_step(NC - 2)
    ring_step(0)
    lax.fori_loop(3, NZ, weight_block, 0)
    rs3_step(NC - 1)
    ring_step(1)
    ring_step(2)

    for j in range(1, TP):
        bstat_in(j).wait_recv()
    for c in range(NC):
        for j in range(3):
            rs3(c, j).wait_recv()
    for h in range(2):
        sums = bst_r[h]
        for j in range(1, TP // 2):
            sums = sums + bst_r[2 * j + h]
        m1 = sums[0:1] / D
        m2 = sums[1:2] / D
        for c in range(NC):
            cols = pl.ds(h * HALF + c * TC, TC)
            rel = slice(c * TC, (c + 1) * TC)
            here = own[c] + r3[c, 0].astype(F32)
            there = r3[c, 1].astype(F32) + r3[c, 2].astype(F32)
            scaled_g = jnp.where(k == h, here, there) * gain_l[...]
            rstd = mr[1:2, cols]
            nhat = (cv[:, cols] - mr[0:1, cols]) * rstd
            gc[:, pl.ds(PAD + h * HALF + c * TC, TC)] = rstd * (
                scaled_g - m1[:, rel] - nhat * m2[:, rel]
            )
    gch_s[0] = gc[:, pl.ds(TOK, PAD)]
    gch_s[1] = gc[:, pl.ds(PAD, PAD)]
    for d in range(2):
        ghalo(d).start()

    ring_step(3)
    ring_step(4)

    gkp[...] = jnp.zeros_like(gkp)
    lane = lax.broadcasted_iota(jnp.int32, (8, 128), 1)

    def tap_rows(i, carry):
        rows = pl.ds(pl.multiple_of(i * 8, 8), 8)
        x = xp[rows, :]
        g = gc[rows, pl.ds(PAD, TOK)]
        total = jnp.zeros((8, 128), F32)
        for tap in range(KW):
            prod = g * shifted(x, tap - REACH)[:, PAD : PAD + TOK]
            total = jnp.where(lane == tap, jnp.sum(prod, axis=1, keepdims=True), total)
        gkp[rows, :] = total
        return carry

    lax.fori_loop(0, W // 8, tap_rows, 0)
    gks[...] = gkp[...].T[0:16, :]
    for j in range(1, SEQ):
        gk_out(j).start()
    gkr[sq] = gks[...]

    ring_step(5)
    ring_step(6)

    for d in range(2):
        ghalo(d).wait_recv()
    gc[:, pl.ds(0, PAD)] = jnp.where(sq == 0, 0.0, gch[0])
    gc[:, pl.ds(PAD + TOK, PAD)] = jnp.where(sq == SEQ - 1, 0.0, gch[1])

    def back_rows(i, carry):
        rows = pl.ds(pl.multiple_of(i * 16, 16), 16)
        g = gc[rows, :]
        t = taps[rows, :]
        total = go_t[rows, :].astype(F32)
        for tap in range(KW):
            total = total + t[:, tap : tap + 1] * shifted(g, REACH - tap)[:, PAD : PAD + TOK]
        gi_t[rows, :] = total.astype(BF)
        return carry

    lax.fori_loop(0, W // 16, back_rows, 0)

    factor = 1.0 / math.sqrt(TOK * SEQ)
    for j in range(1, SEQ):
        gk_in(j).wait_recv()
    total = gkr[0]
    for j in range(1, SEQ):
        total = total + gkr[j]
    gk[...] = total * factor

    ring_step(7)
    x_swap().wait_recv()
    gu[...] = (wf[z, xl, 0] + x_r[0].astype(F32)) * factor
    gd[...] = (wf[z, xl, 1] + x_r[1].astype(F32)) * factor

    for d in range(2):
        halo(d).wait_send()
        ghalo(d).wait_send()
    for i in range(3):
        weight(i).wait_send()
    for j in range(1, TP):
        stat_out(j).wait_send()
        bstat_out(j).wait_send()
    for j in range(1, SEQ):
        gk_out(j).wait_send()

    def drain(c, carry):
        for a in range(2):
            for j in range(3):
                ag1(a, c, j).wait_send()
            for d in range(2):
                ag2(a, c, d).wait_send()
                ag3(a, c, d).wait_send()
        for d in range(2):
            rs1(c, d).wait_send()
            rs2(c, d).wait_send()
        for j in range(3):
            rs3(c, j).wait_send()
        return carry

    lax.fori_loop(0, NC, drain, 0)
    for i in range(NZ):
        core_w(i).wait_send()
    for d in range(2):
        for step in range(4):
            for e in range(2):
                ring(d, step, e).wait_send()
    x_swap().wait_send()


def block(inputs, grad_out, kernel, ln_gain, layer_scale, w_up, w_down):
    start = lax.axis_index("tp") * W
    gain_l = lax.dynamic_slice_in_dim(ln_gain, start, W, 0)[:, None]
    scale_l = lax.dynamic_slice_in_dim(layer_scale, start, W, 0)[:, None]
    dma, vmem = pltpu.SemaphoreType.DMA, pltpu.VMEM
    scratch = [
        vmem((2, NC, W, TC), BF),
        vmem((2, NC, W, TC), BF),
        vmem((NC, D, TC), BF),
        vmem((NC, D, TC), BF),
        vmem((W, TOK + 2 * PAD), F32),
        vmem((W, TOK), F32),
        vmem((2, W, PAD), BF),
        vmem((2, TOK), F32),
        vmem((TP, 2, TOK), F32),
        vmem((2, TOK), F32),
        vmem((D, U), BF),
        vmem((U, D), BF),
        vmem((U, D), BF),
        vmem((U, TC), F32),
        vmem((U, TC), F32),
        vmem((NC, 2 * U, TC), BF),
        vmem((NC, 2 * U, TC), BF),
        vmem((NC, D, TC), F32),
        vmem((2, NC, 2 * W, TC), BF),
        vmem((2, NC, 2 * W, TC), BF),
        vmem((2, NC, 4 * W, TC), BF),
        vmem((2, NC, 4 * W, TC), BF),
        vmem((NC, 3, W, TC), BF),
        vmem((NC, 3, W, TC), BF),
        vmem((NC, W, TC), F32),
        vmem((2, HALF), F32),
        vmem((TP, 2, HALF), F32),
        vmem((W, TOK + 2 * PAD), F32),
        vmem((2, W, PAD), F32),
        vmem((2, W, PAD), F32),
        vmem((128, 128), F32),
        vmem((16, 128), F32),
        vmem((SEQ, 16, 128), F32),
        vmem((NZ, 2, 2, W, U), F32),
        vmem((NZ, 2, 2, W, U), BF),
        vmem((NZ, 2, 2, W, U), BF),
        vmem((2, 4, 2, 2, W, U), BF),
        vmem((2, 4, 2, 2, W, U), BF),
        vmem((2, W, U), BF),
        vmem((2, W, U), BF),
    ]
    for count in (2, 3, TP, 6 * NC, 4 * NC, 4 * NC, 2 * NC, 2 * NC, 3 * NC, TP, 2, SEQ, NZ, 16, 1):
        scratch += [dma((count,)), dma((count,))]
    spec = pl.BlockSpec(memory_space=pltpu.VMEM)
    gi_t, gu, gd, gk = pl.pallas_call(
        body,
        out_shape=[
            jax.ShapeDtypeStruct((W, TOK), BF),
            jax.ShapeDtypeStruct((W, U), F32),
            jax.ShapeDtypeStruct((W, U), F32),
            jax.ShapeDtypeStruct((16, 128), F32),
        ],
        in_specs=[spec] * 9,
        out_specs=[spec] * 4,
        scratch_shapes=scratch,
        compiler_params=pltpu.CompilerParams(
            collective_id=0, has_side_effects=True, vmem_limit_bytes=60 * 2**20
        ),
    )(
        inputs.T, grad_out.T, kernel.T, gain_l, scale_l, ln_gain[:, None], w_up, w_up.T, w_down,
    )
    return gi_t.T, gu, gd, gk[:KW, :W]


def solution(mesh):
    in_specs = (
        P("seq", "tp"),
        P("seq", "tp"),
        P(None, "tp"),
        P(),
        P(),
        P(None, "tp"),
        P("tp", None),
    )
    out_specs = (P("seq", "tp"), P("seq", "tp"), P("seq", "tp"), P(None, "tp"))
    return jax.shard_map(block, mesh=mesh, in_specs=in_specs, out_specs=out_specs, check_vma=False)
```

time: 549 us -> 168 us (0.31)
  waiting for transfers between devices: 282 us -> 0 us
  blocking collectives: 168 us -> 0 us
  Pallas kernels: 0 us -> 154 us
  matrix products: 29.2 us -> 0 us
  other arithmetic: 19.1 us -> 0 us
  starting transfers between devices: 15.8 us -> 0 us
  between operations: 14 us -> 0.66 us
  local copies, waits for them, and re-layouts: 20.2 us -> 12.6 us
    psum x3 -> x0, blocking collectives: 168 us -> none  [the longest x1 67.7 us: local(): lax.psum((jnp.sum(conv, axis=1), jnp.sum(conv * conv, axis=1)), 'tp')]
    pallas_call x0 -> x1, Pallas kernels: none -> 154 us  [block(): pl.pallas_call(body, out_shape=[jax.ShapeDtypeStruct((W, TOK), BF), jax.S...]
    all_gather x2 -> x0, waiting for transfers between devices: 121 us -> none  [the longest x1 61.9 us: local(): lax.all_gather(grad_out, 'tp', axis=1, tiled=True)]
    reduce_scatter x1 -> x0, waiting for transfers between devices: 95 us -> none  [local(): lax.psum_scatter(contract_last(w_up, grad_pre).astype(jnp.bfloat16), 'tp'...]
    unnamed x5 -> x0, waiting for transfers between devices: 58.2 us -> none
    dot_general x5 -> x0, matrix products: 29.2 us -> none  [the longest x2 11.7 us: contract_last(): lax.dot_general(left, right, (((1,), (1,)), ((), ())), preferred_element_...]
    ppermute x4 -> x0, starting transfers between devices: 15.5 us -> none  [the longest x2 9.64 us: extended(): lax.ppermute(head, axis, [((i + 1) % count, i) for i in range(ends)])]
    reduce_sum x4 -> x0, other arithmetic: 10.9 us -> none  [the longest x1 4.99 us: local(): jnp.sum(grad_conv * padded[offset:offset + positions], axis=0)]
  transfers between devices with their start and end apart: 8 -> 0, of which waited for: 6 -> 0; matrix products, arithmetic and copies ran while one was open for 5% -> 0% of each run, Pallas kernels for 0% -> 0%
where the time goes in v1:
time: 168 us; the launch traced here: 167 us
  Pallas kernels  154 us (92%)
  local copies, waits for them, and re-layouts  12.6 us (8%)
    pallas_call x1, Pallas kernels, block(): pl.pallas_call(body, out_shape=[jax.ShapeDtypeStruct((W, TOK), BF), jax.S...  154 us
    unnamed x10, local copies, waits for them, and re-layouts  8.49 us

profile of v1, /device:TPU:2, one launch (start us, length us, event | category | flops | bytes accessed | tf_op | source)
XLA Modules:
  0.0 167.1 jit_solution(16716822509836907408)
XLA Ops:
  0.6 0.8 dynamic-slice_bitcast_fusion
  1.4 0.7 copy.18.scale_l
  2.2 0.7 copy.17.gain_l
  2.9 1.4 copy.15
  4.3 1.9 %broadcast_in_dim.12.gain_all = f32[1536,1]{1,0:T(8,128)} reshape(f32[1536]{0:T(1024)} %param.10) | data formatting | bytes 12288 | tf_op jit(solution)/shard_map/broadcast_in_dim | solution.py:584
  6.2 2.4 %copy.16 = bf16[1536,384]{0,1:T(8,128)(2,1)} copy(bf16[1536,384]{1,0:T(8,128)(2,1)} %wu.1) | data formatting | bytes 2359296 | tf_op args[5]
  8.6 153.8 %shard_map.102 = (bf16[96,2048]{1,0:T(8,128)(2,1)}, f32[96,384]{1,0:T(8,128)}, f32[96,384]{1,0:T(8,128)}, f32[16,128]{1,0:T(8,128)}) custom-call(bf16[96,2048]{1,0:T(8,128)(2,1)} %bitcast.11, bf16[96,2048]{1,0:T(8,128)(2,1)} %bitcast.12, f32[96,15]{1,0:T(8,128)} %bitcast.14, f32[96,1]{1,0:T(8,128)} %copy.17.gain_l, f32[96,1]{1,0:T(8,128)} %copy.18.scale_l, ...), custom_call_target="tpu_custom_call" | custom-call | tf_op jit(solution)/shard_map/pallas_call | solution.py:569
  162.4 0.0 copy-start
  162.4 0.0 copy-start.1
  162.4 1.8 %copy.24 = bf16[2048,96]{0,1:T(8,128)(2,1)} copy(bf16[2048,96]{0,1:T(8,128)(2,1)} %bitcast.13) | data formatting | bytes 786432
  164.2 1.6 copy.25
  165.8 0.0 copy-done
  165.8 0.7 copy.26
  166.5 0.0 copy-done.1
  166.5 0.6 copy.27
Async XLA Ops:
  162.4 3.4 %copy-start = (f32[96,384]{1,0:T(8,128)S(1)}, f32[96,384]{1,0:T(8,128)}, u32[]{:S(2)}) copy-start(f32[96,384]{1,0:T(8,128)} %get-tuple-element.20) | copy-start | bytes 442372
  162.4 4.1 %copy-start.1 = (f32[16,128]{1,0:T(8,128)S(1)}, f32[16,128]{1,0:T(8,128)}, u32[]{:S(2)}) copy-start(f32[16,128]{1,0:T(8,128)} %get-tuple-element.11) | copy-start | bytes 24580

commit v2 on v1

v2 whole, which is shorter than its diff:
```python
import math

import jax
import jax.numpy as jnp
from jax import lax
from jax.experimental import pallas as pl
from jax.experimental.pallas import tpu as pltpu
from jax.sharding import PartitionSpec as P

MESH = pl.DeviceIdType.MESH
BF = jnp.bfloat16
F32 = jnp.float32

TP = 16
NY = 4
SEQ = 16
NZ = 8
W = 96
D = 1536
TOK = 2048
HALF = TOK // 2
NC = 4
TC = HALF // NC
U = 384
KW = 15
EDGE = 8
ROWS = 128

X_FIRST = ((False, True, True, True), (True, False, False, True))


def nn(a, b):
    return jnp.dot(a, b, preferred_element_type=F32)


def nt(a, b):
    return lax.dot_general(a, b, (((1,), (1,)), ((), ())), preferred_element_type=F32)


def body(
    x_in, go, taps, gain, scale, wu, wd,
    gi, gu, gd, gk,
    s_st, n_st, g_s, g_n, xp, cv, hin, st_s, st_1, st_m, st_2, mr, cols, gb, wu_t, wu_p, wu_tp,
    wd_p, pre_s, gh_s, hid, gpr, pf, s1, r1, s2, r2, s3, r3, own, bst, b_1, b_m, b_2, gc, gch,
    gks, gk_1, gk_m, gk_2, wf, c_s, c_r, z_s, z_r, x_s, x_r,
    halo_ss, halo_rs, w_ss, w_rs, st_ss, st_rs, ag_ss, ag_rs,
    r1_ss, r1_rs, r2_ss, r2_rs, r3_ss, r3_rs, b_ss, b_rs, gh_ss, gh_rs, gk_ss, gk_rs,
    c_ss, c_rs, z_ss, z_rs, x_ss, x_rs,
):
    tp = lax.axis_index("tp")
    sq = lax.axis_index("seq")
    k = lax.rem(tp, 2)
    xh = lax.rem(tp // 2, 2)
    y = tp // 4
    xl = sq // NZ
    z = lax.rem(sq, NZ)
    sent = []

    def at(y_, xh_, k_):
        return {"seq": sq, "tp": (y_ * 2 + xh_) * 2 + k_}

    def send(src, dst, ss, rs, dev):
        return pltpu.make_async_remote_copy(
            src_ref=src, dst_ref=dst, send_sem=ss, recv_sem=rs, device_id=dev, device_id_type=MESH
        )

    def go_out(copy):
        copy.start()
        sent.append(copy)

    up, down = lax.rem(y + 1, NY), lax.rem(y + NY - 1, NY)
    anti = lax.rem(y + 2, NY)
    y_dev = (at(up, xh, k), at(down, xh, k), at(anti, xh, k))
    other = 1 - k
    near = (at(y, 1 - xh, k), at(y, xh, other), at(y, 1 - xh, other))
    sq_next, sq_prev = lax.rem(sq + 1, SEQ), lax.rem(sq + SEQ - 1, SEQ)
    sq_dev = ({"seq": sq_next, "tp": tp}, {"seq": sq_prev, "tp": tp})
    z_dev = [{"seq": xl * NZ + lax.rem(z + j, NZ), "tp": tp} for j in range(NZ)]
    z_ring = (z_dev[1], z_dev[NZ - 1])
    x_dev = {"seq": (1 - xl) * NZ + z, "tp": tp}

    def rows_at(first, count):
        return pl.ds(pl.multiple_of(first, 32), count)

    def y_rows(which, first=0, count=4 * W):
        return rows_at(which * (4 * W) + first, count)

    def pair_rows(which, first=0, count=2 * W):
        return rows_at(which * (4 * W) + xh * (2 * W) + first, count)

    my_rows = rows_at(tp * W, W)

    barrier = pltpu.get_barrier_semaphore()
    partners = [*near, *y_dev, *sq_dev, *z_dev[1:], x_dev]
    for dev in partners:
        pl.semaphore_signal(barrier, inc=1, device_id=dev, device_id_type=MESH)

    def halo(d):
        src = x_in.at[pl.ds(TOK - 16, 16)] if d == 0 else x_in.at[pl.ds(0, 16)]
        return send(src, hin.at[d], halo_ss.at[d], halo_rs.at[d], sq_dev[d])

    def weight(i):
        src, dst = ((wd, wd_p), (wu, wu_p), (wu_t, wu_tp))[i]
        return send(src, dst, w_ss.at[i], w_rs.at[i], near[1])

    def stat(stage, j):
        src, dst, dev = ((st_s, st_1, near), (st_m, st_2, y_dev))[stage]
        i = stage * 3 + j
        return send(src, dst.at[j], st_ss.at[i], st_rs.at[i], dev[j])

    def bstat(stage, j):
        src, dst, dev = ((bst, b_1, y_dev), (b_m, b_2, near))[stage]
        i = stage * 3 + j
        return send(src, dst.at[j], b_ss.at[i], b_rs.at[i], dev[j])

    staged, full = (s_st, n_st), (g_s, g_n)

    def gather(a, c, slot):
        i = (a * NC + c) * 10 + slot
        buf = full[a].at[c]
        if slot < 3:
            src = staged[a].at[k if slot == 0 else other, c]
            return send(src, buf.at[my_rows], ag_ss.at[i], ag_rs.at[i], near[slot])
        if X_FIRST[a][c]:
            part, dev = (
                (y_rows(y), y_dev[0]),
                (y_rows(y), y_dev[1]),
                (y_rows(down, 0, 2 * W), y_dev[0]),
                (y_rows(up, 2 * W, 2 * W), y_dev[1]),
            )[slot - 3]
        else:
            part, dev = (
                (pair_rows(y), y_dev[0]),
                (pair_rows(y), y_dev[1]),
                (pair_rows(down, 0, W), y_dev[0]),
                (pair_rows(up, W, W), y_dev[1]),
                (pair_rows(y), near[0]),
                (pair_rows(down), near[0]),
                (pair_rows(up), near[0]),
            )[slot - 3]
        part = buf.at[part]
        return send(part, part, ag_ss.at[i], ag_rs.at[i], dev)

    def gather_last(a, c, d):
        i = (a * NC + c) * 2 + d
        part = full[a].at[c].at[pair_rows(anti, d * W, W)]
        i = 2 * NC * 10 + i
        return send(part, part, ag_ss.at[i], ag_rs.at[i], near[0])

    def gather_0(a, c):
        for slot in (2, 0, 1) if X_FIRST[a][c] else (1,):
            go_out(gather(a, c, slot))
        full[a][c, my_rows] = staged[a][k, c]

    def gather_1(a, c):
        for slot in (2, 0, 1) if X_FIRST[a][c] else (1,):
            gather(a, c, slot).wait_recv()
        go_out(gather(a, c, 3))
        go_out(gather(a, c, 4))
        if not X_FIRST[a][c]:
            go_out(gather(a, c, 7))

    def gather_2(a, c):
        for d in range(2):
            gather(a, c, 3 + d).wait_recv()
            go_out(gather(a, c, 5 + d))
            if not X_FIRST[a][c]:
                go_out(gather(a, c, 8 + d))

    def gather_3(a, c):
        if not X_FIRST[a][c]:
            for d in range(2):
                gather(a, c, 5 + d).wait_recv()
                go_out(gather_last(a, c, d))

    def gather_end(a, c):
        if X_FIRST[a][c]:
            for d in range(2):
                gather(a, c, 5 + d).wait_recv()
        else:
            for slot in (7, 8, 9):
                gather(a, c, slot).wait_recv()
            for d in range(2):
                gather_last(a, c, d).wait_recv()

    def rs1(c, d):
        i = c * 2 + d
        return send(s1.at[d, c], r1.at[d, c], r1_ss.at[i], r1_rs.at[i], y_dev[d])

    def rs2(c, d):
        i = c * 2 + d
        return send(s2.at[d, c], r2.at[d, c], r2_ss.at[i], r2_rs.at[i], y_dev[d])

    def rs3(c, j):
        i = c * 3 + j
        return send(s3.at[c, j], r3.at[c, j], r3_ss.at[i], r3_rs.at[i], near[j])

    def ghalo(d):
        src = gc.at[pl.ds(TOK, EDGE)] if d == 0 else gc.at[pl.ds(EDGE, EDGE)]
        return send(src, gch.at[d], gh_ss.at[d], gh_rs.at[d], sq_dev[d])

    def gk_x():
        return send(gks, gk_1, gk_ss.at[0], gk_rs.at[0], x_dev)

    def gk_z(j):
        return send(gk_m, gk_2.at[j], gk_ss.at[j], gk_rs.at[j], z_dev[j])

    def core_w(i):
        return send(c_s.at[i], c_r.at[i], c_ss.at[i], c_rs.at[i], near[1])

    def ring(d, step, e):
        i = (d * 4 + step) * 2 + e
        if step == 0:
            return send(
                z_s.at[d, step, e, pl.ds(d, 1)], z_r.at[d, step, e, pl.ds(d, 1)],
                z_ss.at[i], z_rs.at[i], z_ring[d],
            )
        return send(z_s.at[d, step, e], z_r.at[d, step, e], z_ss.at[i], z_rs.at[i], z_ring[d])

    def x_swap():
        return send(x_s, x_r, x_ss.at[0], x_rs.at[0], x_dev)

    turn = lax.rem(D - tp * W, D)
    scale_row = pltpu.roll(jnp.broadcast_to(scale[...], (8, D)), turn, 1)[0:1, 0:W]
    gain_row = pltpu.roll(jnp.broadcast_to(gain[...], (8, D)), turn, 1)[0:1, 0:128]
    cols[...] = jnp.broadcast_to(gain_row, (128, 128)).T
    for c in range(NC):
        for h in range(2):
            rows = pl.ds(h * HALF + c * TC, TC)
            s_st[h, c] = (scale_row * go[rows, :].astype(F32)).T.astype(BF)

    pl.semaphore_wait(barrier, len(partners))
    for d in range(2):
        go_out(halo(d))
    for c in range(NC):
        gather_0(0, c)
    for i in range(2):
        go_out(weight(i))

    def load(i, carry):
        xp[pl.ds(pl.multiple_of(EDGE + i * ROWS, 8), ROWS), :] = x_in[
            pl.ds(pl.multiple_of(i * ROWS, ROWS), ROWS), :
        ].astype(F32)
        return carry

    lax.fori_loop(0, TOK // ROWS, load, 0)
    for d in range(2):
        halo(d).wait_recv()
    xp[0:EDGE, :] = jnp.where(sq == 0, 0.0, hin[0].astype(F32)[8:16])
    xp[pl.ds(EDGE + TOK, EDGE), :] = jnp.where(sq == SEQ - 1, 0.0, hin[1].astype(F32)[0:8])

    def conv_rows(i, carry):
        total = None
        for tap in range(KW):
            term = taps[tap : tap + 1, :] * xp[pl.ds(i * ROWS + tap + 1, ROWS), :]
            total = term if total is None else total + term
        out = total.T
        at_ = pl.ds(pl.multiple_of(i * ROWS, ROWS), ROWS)
        cv[:, at_] = out
        st_s[0:1, at_] = jnp.sum(out, axis=0, keepdims=True)
        st_s[1:2, at_] = jnp.sum(out * out, axis=0, keepdims=True)
        return carry

    lax.fori_loop(0, TOK // ROWS, conv_rows, 0)
    for j in range(3):
        go_out(stat(0, j))
    gather_1(0, 0)
    for j in range(3):
        stat(0, j).wait_recv()
    st_m[...] = (st_s[...] + st_1[1]) + (st_1[0] + st_1[2])
    for j in range(3):
        go_out(stat(1, j))
    gather_1(0, 1)
    for j in range(3):
        stat(1, j).wait_recv()
    totals = (st_m[...] + st_2[2]) + (st_2[0] + st_2[1])
    mean = totals[0:1] / D
    var = totals[1:2] / D - mean * mean
    mr[0:1, :] = mean
    mr[1:2, :] = lax.rsqrt(var + 1e-06)
    gain_col = cols[0:W, 0:1]
    for c in range(NC):
        for h in range(2):
            at_ = pl.ds(h * HALF + c * TC, TC)
            nhat = (cv[:, at_] - mr[0:1, at_]) * mr[1:2, at_]
            n_st[h, c] = (nhat * gain_col).astype(BF)
        gather_0(1, c)

    for c in range(2, NC):
        gather_1(0, c)

    for i in range(D // 128):
        part = slice(i * 128, (i + 1) * 128)
        wu_t[:, part] = wu[part, :].T
        gb[part, :] = jnp.broadcast_to(gain[0:1, part], (128, 128)).T
    go_out(weight(2))

    gather_2(0, 0)
    gather_1(1, 0)
    gather_2(0, 1)
    gather_1(1, 1)
    gather_3(0, 0)
    gather_2(0, 2)
    gather_1(1, 2)
    gather_2(0, 3)
    gather_1(1, 3)
    for i in range(3):
        weight(i).wait_recv()

    def cotangent(c):
        gather_end(0, c)
        gh_s[c, 0:U] = nn(wd[...], g_s[c])
        gh_s[c, U:] = nn(wd_p[...], g_s[c])

    def rs2_step(c):
        for d, to in ((0, up), (1, down)):
            rs1(c, d).wait_recv()
            a, b = d * 2 * W, (1 - d) * 2 * W
            got = pf[c, y_rows(to, a, 2 * W)] + r1[d, c].astype(F32)
            s2[d, c, pl.ds(a, 2 * W)] = got.astype(BF)
            s2[d, c, pl.ds(b, 2 * W)] = pf[c, y_rows(to, b, 2 * W)].astype(BF)
            go_out(rs2(c, d))

    def rs3_step(c):
        for d in range(2):
            rs2(c, d).wait_recv()

        def group(g):
            rows = rows_at(g * W, W)
            mine = pf[c, y_rows(y, g * W, W)]
            return mine + r2[0, c, rows].astype(F32) + r2[1, c, rows].astype(F32)

        for j, (xh_, k_) in ((2, (1 - xh, other)), (0, (1 - xh, k)), (1, (xh, other))):
            s3[c, j] = group(xh_ * 2 + k_).astype(BF)
            go_out(rs3(c, j))
        own[c] = group(xh * 2 + k)

    def layers(c):
        at_ = pl.ds(c * TC, TC)
        acc = jnp.zeros((8, TC), F32)
        for u, w_t in enumerate((wu_t, wu_tp)):
            pre_s[...] = nn(w_t[...], g_n[c])

            def act(i, acc, u=u):
                v = pre_s[rows_at(i * 32, 32), :]
                to = rows_at(u * U + i * 32, 32)
                phi = 0.5 + 0.5 * lax.erf(v * 0.7071067811865476)
                slope = phi + v * jnp.exp(-0.5 * v * v) * 0.3989422804014327
                gp = (gh_s[c, to] * slope).astype(BF)
                hid[to, at_] = (v * phi).astype(BF)
                gpr[to, at_] = gp
                return acc + jnp.sum((gp.astype(F32) * v).reshape(4, 8, TC), axis=0)

            acc = lax.fori_loop(0, U // 32, act, acc)
        bst[1:2, at_] = jnp.sum(acc, axis=0, keepdims=True)

    def back(c):
        at_ = pl.ds(c * TC, TC)
        acc = [jnp.zeros((8, 128), F32)] * (TC // 128)
        for r in range(NY):
            rows = pl.ds(r * 4 * W, 4 * W)
            p = nn(wu[rows, :], gpr[0:U, at_]) + nn(wu_p[rows, :], gpr[U:, at_])
            pf[c, rows] = p
            for h in range(TC // 128):
                term = gb[rows, :] * p[:, h * 128 : (h + 1) * 128]
                acc[h] = acc[h] + jnp.sum(term.reshape(4 * W // 8, 8, 128), axis=0)
        for h in range(TC // 128):
            bst[0:1, pl.ds(c * TC + h * 128, 128)] = jnp.sum(acc[h], axis=0, keepdims=True)
        for d in range(2):
            s1[d, c] = pf[c, y_rows(anti, d * 2 * W, 2 * W)].astype(BF)
            go_out(rs1(c, d))

    cotangent(0)
    cotangent(1)
    gather_2(1, 0)
    cotangent(2)
    gather_2(1, 1)
    gather_3(1, 0)
    cotangent(3)
    gather_end(1, 0)
    layers(0)
    gather_3(1, 1)
    gather_2(1, 2)
    back(0)
    gather_2(1, 3)
    gather_end(1, 1)
    layers(1)
    gather_3(1, 2)
    back(1)
    rs2_step(0)
    gather_3(1, 3)
    gather_end(1, 2)
    layers(2)
    rs3_step(0)
    back(2)
    rs2_step(1)
    gather_end(1, 3)
    layers(3)
    back(3)
    for j in range(3):
        go_out(bstat(0, j))

    order = (4, 3, 5, 2, 6, 1, 7, 0)

    def weight_blocks(first, count):
        for a, (left, right) in enumerate(((g_n, gpr), (g_s, hid))):
            wide = []
            for c in range(NC):
                pieces = []
                for i in range(count):
                    b = lax.rem(z + order_at(first, i), NZ)
                    for e in range(2):
                        pieces.append(left[c, rows_at(e * (NZ * W) + b * W, W), :])
                wide.append(jnp.concatenate(pieces, axis=0))
            lhs = jnp.concatenate(wide, axis=1)
            theirs = nt(lhs, right[U:, :])
            mine = nt(lhs, right[0:U, :])
            for i in range(count):
                b = lax.rem(z + order_at(first, i), NZ)
                for e in range(2):
                    part = slice((i * 2 + e) * W, (i * 2 + e + 1) * W)
                    c_s[first + i, e, a] = theirs[part].astype(BF)
                    wf[b, e, a] = mine[part]
        for i in range(count):
            core_w(first + i).start()

    def order_at(first, i):
        return order[first + i]

    def ring_step(i):
        off = order[i]
        b = lax.rem(z + off, NZ)
        core_w(i).wait_recv()
        if off == 4:
            for e in range(2):
                for d in range(2):
                    got = wf[b, e, d] + c_r[i, e, d].astype(F32)
                    z_s[d, 0, e, d] = got.astype(BF)
                    go_out(ring(d, 0, e))
        elif off != 0:
            d = 0 if off < 4 else 1
            step = 4 - off if off < 4 else off - 4
            for e in range(2):
                ring(d, step - 1, e).wait_recv()
                for a in range(2):
                    got = wf[b, e, a] + c_r[i, e, a].astype(F32)
                    if step > 1 or a == d:
                        got = got + z_r[d, step - 1, e, a].astype(F32)
                    z_s[d, step, e, a] = got.astype(BF)
                go_out(ring(d, step, e))
        else:
            for e in range(2):
                for d in range(2):
                    ring(d, 3, e).wait_recv()

            def part(e, a):
                got = wf[b, e, a] + c_r[i, e, a].astype(F32)
                return got + z_r[0, 3, e, a].astype(F32) + z_r[1, 3, e, a].astype(F32)

            for a in range(2):
                x_s[a] = part(1 - xl, a).astype(BF)
            go_out(x_swap())
            for a in range(2):
                wf[b, xl, a] = part(xl, a)

    weight_blocks(0, 1)
    rs3_step(1)
    rs2_step(2)
    weight_blocks(1, 2)
    ring_step(0)
    rs2_step(3)
    rs3_step(2)
    ring_step(1)
    ring_step(2)
    weight_blocks(3, 2)
    for j in range(3):
        bstat(0, j).wait_recv()
    b_m[...] = (bst[...] + b_1[2]) + (b_1[0] + b_1[1])
    for j in range(3):
        go_out(bstat(1, j))
    rs3_step(3)
    weight_blocks(5, 3)
    ring_step(3)
    ring_step(4)

    for j in range(3):
        bstat(1, j).wait_recv()
    for c in range(NC):
        for j in range(3):
            rs3(c, j).wait_recv()
    sums_here = (b_m[...] + b_2[0]) / D
    sums_there = (b_2[1] + b_2[2]) / D
    for h in range(2):
        sums = jnp.where(k == h, sums_here, sums_there)
        for c in range(NC):
            at_ = pl.ds(h * HALF + c * TC, TC)
            rel = slice(c * TC, (c + 1) * TC)
            here = own[c] + r3[c, 0].astype(F32)
            there = r3[c, 1].astype(F32) + r3[c, 2].astype(F32)
            scaled_g = jnp.where(k == h, here, there) * gain_col
            rstd = mr[1:2, at_]
            nhat = (cv[:, at_] - mr[0:1, at_]) * rstd
            grad = rstd * (scaled_g - sums[0:1, rel] - nhat * sums[1:2, rel])
            gc[pl.ds(EDGE + h * HALF + c * TC, TC), :] = grad.T
    for d in range(2):
        go_out(ghalo(d))

    def tap_rows(i, sums):
        g = gc[pl.ds(pl.multiple_of(EDGE + i * ROWS, 8), ROWS), :]
        out = []
        for tap in range(KW):
            prod = g * xp[pl.ds(i * ROWS + tap + 1, ROWS), :]
            out.append(sums[tap] + jnp.sum(prod.reshape(ROWS // 8, 8, W), axis=0))
        return tuple(out)

    sums = lax.fori_loop(0, TOK // ROWS, tap_rows, (jnp.zeros((8, W), F32),) * KW)
    for tap in range(KW):
        gks[tap : tap + 1, :] = jnp.sum(sums[tap], axis=0, keepdims=True)
    gks[KW : KW + 1, :] = jnp.zeros((1, W), F32)
    go_out(gk_x())

    ring_step(5)
    ring_step(6)

    gk_x().wait_recv()
    gk_m[...] = gks[...] + gk_1[...]
    for j in range(1, NZ):
        go_out(gk_z(j))
    for d in range(2):
        ghalo(d).wait_recv()
    gc[0:EDGE, :] = jnp.where(sq == 0, 0.0, gch[0])
    gc[pl.ds(EDGE + TOK, EDGE), :] = jnp.where(sq == SEQ - 1, 0.0, gch[1])

    def back_rows(i, carry):
        at_ = pl.ds(pl.multiple_of(i * ROWS, ROWS), ROWS)
        total = go[at_, :].astype(F32)
        for tap in range(KW):
            total = total + taps[tap : tap + 1, :] * gc[pl.ds(i * ROWS + KW - tap, ROWS), :]
        gi[at_, :] = total.astype(BF)
        return carry

    lax.fori_loop(0, TOK // ROWS, back_rows, 0)

    factor = 1.0 / math.sqrt(TOK * SEQ)
    total = gk_m[...]
    for j in range(1, NZ):
        gk_z(j).wait_recv()
        total = total + gk_2[j]
    gk[...] = total[0:KW] * factor

    ring_step(7)
    x_swap().wait_recv()
    gu[...] = (wf[z, xl, 0] + x_r[0].astype(F32)) * factor
    gd[...] = (wf[z, xl, 1] + x_r[1].astype(F32)) * factor

    for copy in sent:
        copy.wait_send()
    for i in range(NZ):
        core_w(i).wait_send()


def block(inputs, grad_out, kernel, ln_gain, layer_scale, w_up, w_down):
    dma, vmem = pltpu.SemaphoreType.DMA, pltpu.VMEM
    scratch = [
        vmem((2, NC, W, TC), BF),
        vmem((2, NC, W, TC), BF),
        vmem((NC, D, TC), BF),
        vmem((NC, D, TC), BF),
        vmem((TOK + 2 * EDGE, W), F32),
        vmem((W, TOK), F32),
        vmem((2, 16, W), BF),
        vmem((2, TOK), F32),
        vmem((3, 2, TOK), F32),
        vmem((2, TOK), F32),
        vmem((3, 2, TOK), F32),
        vmem((2, TOK), F32),
        vmem((128, 128), F32),
        vmem((D, 128), F32),
        vmem((U, D), BF),
        vmem((D, U), BF),
        vmem((U, D), BF),
        vmem((U, D), BF),
        vmem((U, TC), F32),
        vmem((NC, 2 * U, TC), F32),
        vmem((2 * U, HALF), BF),
        vmem((2 * U, HALF), BF),
        vmem((NC, D, TC), F32),
        vmem((2, NC, 2 * W, TC), BF),
        vmem((2, NC, 2 * W, TC), BF),
        vmem((2, NC, 4 * W, TC), BF),
        vmem((2, NC, 4 * W, TC), BF),
        vmem((NC, 3, W, TC), BF),
        vmem((NC, 3, W, TC), BF),
        vmem((NC, W, TC), F32),
        vmem((2, HALF), F32),
        vmem((3, 2, HALF), F32),
        vmem((2, HALF), F32),
        vmem((3, 2, HALF), F32),
        vmem((TOK + 2 * EDGE, W), F32),
        vmem((2, EDGE, W), F32),
        vmem((16, W), F32),
        vmem((16, W), F32),
        vmem((16, W), F32),
        vmem((NZ, 16, W), F32),
        vmem((NZ, 2, 2, W, U), F32),
        vmem((NZ, 2, 2, W, U), BF),
        vmem((NZ, 2, 2, W, U), BF),
        vmem((2, 4, 2, 2, W, U), BF),
        vmem((2, 4, 2, 2, W, U), BF),
        vmem((2, W, U), BF),
        vmem((2, W, U), BF),
    ]
    for count in (2, 3, 6, 24 * NC, 2 * NC, 2 * NC, 3 * NC, 6, 2, NZ, NZ, 16, 1):
        scratch += [dma((count,)), dma((count,))]
    spec = pl.BlockSpec(memory_space=pltpu.VMEM)
    return pl.pallas_call(
        body,
        out_shape=[
            jax.ShapeDtypeStruct((TOK, W), BF),
            jax.ShapeDtypeStruct((W, U), F32),
            jax.ShapeDtypeStruct((W, U), F32),
            jax.ShapeDtypeStruct((KW, W), F32),
        ],
        in_specs=[spec] * 7,
        out_specs=[spec] * 4,
        scratch_shapes=scratch,
        compiler_params=pltpu.CompilerParams(
            collective_id=0, has_side_effects=True, vmem_limit_bytes=60 * 2**20
        ),
    )(inputs, grad_out, kernel, ln_gain[None, :], layer_scale[None, :], w_up, w_down)


def solution(mesh):
    in_specs = (
        P("seq", "tp"),
        P("seq", "tp"),
        P(None, "tp"),
        P(),
        P(),
        P(None, "tp"),
        P("tp", None),
    )
    out_specs = (P("seq", "tp"), P("seq", "tp"), P("seq", "tp"), P(None, "tp"))
    return jax.shard_map(block, mesh=mesh, in_specs=in_specs, out_specs=out_specs, check_vma=False)
```

time: 168 us -> 136 us (0.81)
  Pallas kernels: 154 us -> 124 us
  local copies, waits for them, and re-layouts: 12.6 us -> 10.5 us
    pallas_call x1, Pallas kernels: 154 us -> 124 us  [block(): pl.pallas_call(body, out_shape=[jax.ShapeDtypeStruct((TOK, W), BF), jax.S...]
    unnamed x10 -> x11, local copies, waits for them, and re-layouts: 8.49 us -> 5.84 us
    pallas_call x0 -> x1, local copies, waits for them, and re-layouts: none -> 2.02 us  [block(): pl.pallas_call(body, out_shape=[jax.ShapeDtypeStruct((TOK, W), BF), jax.S...]
    broadcast_in_dim x4 -> x2, local copies, waits for them, and re-layouts: 4.13 us -> 2.64 us  [the longest x1 1.34 us: block(): ln_gain[None, :]]
where the time goes in v2:
time: 136 us; the launch traced here: 135 us
  Pallas kernels  124 us (91%)
  local copies, waits for them, and re-layouts  10.5 us (8%)
    pallas_call x1, Pallas kernels, block(): pl.pallas_call(body, out_shape=[jax.ShapeDtypeStruct((TOK, W), BF), jax.S...  124 us
    unnamed x11, local copies, waits for them, and re-layouts  5.84 us

profile of v2, /device:TPU:2, one launch (start us, length us, event | category | flops | bytes accessed | tf_op | source)
XLA Modules:
  0.0 134.9 jit_solution(18292099955804859005)
XLA Ops:
  0.6 0.0 copy-start
  0.6 1.3 broadcast_in_dim.6.gain
  2.0 1.3 broadcast_in_dim.7.scale
  3.3 2.0 %copy.11.x_in = bf16[2048,96]{1,0:T(8,128)(2,1)} copy(bf16[2048,96]{0,1:T(8,128)(2,1)} %param.7) | data formatting | bytes 786432 | tf_op args[0]
  5.3 0.0 copy-done
  5.3 1.0 copy.12.go
  6.3 123.7 %shard_map.102 = (bf16[2048,96]{1,0:T(8,128)(2,1)}, f32[96,384]{1,0:T(8,128)}, f32[96,384]{1,0:T(8,128)}, f32[15,96]{1,0:T(8,128)}) custom-call(bf16[2048,96]{1,0:T(8,128)(2,1)} %copy.11.x_in, bf16[2048,96]{1,0:T(8,128)(2,1)} %copy.12.go, f32[15,96]{1,0:T(8,128)} %taps.1, f32[1,1536]{1,0:T(1,128)} %broadcast_in_dim.6.gain, f32[1,1536]{1,0:T(1,128)} %broadcast_in_dim.7.scale, ...), custom_call_target="tpu_custom_call" | custom-call | tf_op jit(solution)/shard_map/pallas_call | solution.py:616
  130.0 0.0 copy-start.1
  130.0 0.0 copy-start.2
  130.0 2.0 %copy.13 = bf16[2048,96]{0,1:T(8,128)(2,1)} copy(bf16[2048,96]{1,0:T(8,128)(2,1)} %get-tuple-element.4) | data formatting | bytes 786432 | tf_op jit(solution)/shard_map/pallas_call | solution.py:616
  132.1 1.6 %copy.17 = f32[96,384]{1,0:T(8,128)} copy(f32[96,384]{1,0:T(8,128)} %get-tuple-element.13) | data formatting | bytes 294912
  133.6 0.0 copy-done.1
  133.6 0.7 copy.18
  134.3 0.0 copy-done.2
  134.3 0.6 copy.19
Async XLA Ops:
  0.6 4.6 %copy-start = (bf16[2048,96]{0,1:T(8,128)(2,1)S(1)}, bf16[2048,96]{0,1:T(8,128)(2,1)}, u32[]{:S(2)}) copy-start(bf16[2048,96]{0,1:T(8,128)(2,1)} %param.8) | copy-start | bytes 1179652
  130.0 3.6 %copy-start.1 = (f32[96,384]{1,0:T(8,128)S(1)}, f32[96,384]{1,0:T(8,128)}, u32[]{:S(2)}) copy-start(f32[96,384]{1,0:T(8,128)} %get-tuple-element.14) | copy-start | bytes 442372
  130.0 4.3 %copy-start.2 = (f32[15,96]{1,0:T(8,128)S(1)}, f32[15,96]{1,0:T(8,128)}, u32[]{:S(2)}) copy-start(f32[15,96]{1,0:T(8,128)} %get-tuple-element.15) | copy-start | bytes 17284

commit v3 on v2

--- a/solution.py
+++ b/solution.py
@@ -26,7 +26,7 @@
 EDGE = 8
 ROWS = 128
 
-X_FIRST = ((False, True, True, True), (True, False, False, True))
+X_FIRST = ((False, True, False, True), (True, False, True, True))
 
 
 def nn(a, b):
@@ -38,14 +38,14 @@
 
 
 def body(
-    x_in, go, taps, gain, scale, wu, wd,
-    gi, gu, gd, gk,
-    s_st, n_st, g_s, g_n, xp, cv, hin, st_s, st_1, st_m, st_2, mr, cols, gb, wu_t, wu_p, wu_tp,
-    wd_p, pre_s, gh_s, hid, gpr, pf, s1, r1, s2, r2, s3, r3, own, bst, b_1, b_m, b_2, gc, gch,
-    gks, gk_1, gk_m, gk_2, wf, c_s, c_r, z_s, z_r, x_s, x_r,
+    x_t, go_t, taps, gain, scale, wu_hbm, wd_hbm,
+    gi_t, gu, gd, gk,
+    s_st, n_st, g_s, g_n, xp, cv, h_st, hin, st_s, st_1, st_m, st_2, mr, cols, gb, wu, wd, wu_t, wu_p, wu_tp,
+    wd_p, pre_s, hid, gpr, pf, s1, r1, s2, r2, s3, r3, own, bst, b_1, b_m, b_2, gc, gch,
+    gks, gk_1, gk_m, gk_2, wf, c_s, c_r, z_s, z_r, x_s, x_r, e_s, e_r,
     halo_ss, halo_rs, w_ss, w_rs, st_ss, st_rs, ag_ss, ag_rs,
     r1_ss, r1_rs, r2_ss, r2_rs, r3_ss, r3_rs, b_ss, b_rs, gh_ss, gh_rs, gk_ss, gk_rs,
-    c_ss, c_rs, z_ss, z_rs, x_ss, x_rs,
+    c_ss, c_rs, z_ss, z_rs, x_ss, x_rs, e_ss, e_rs, in_ss, _,
 ):
     tp = lax.axis_index("tp")
     sq = lax.axis_index("seq")
@@ -92,12 +92,18 @@
 
     barrier = pltpu.get_barrier_semaphore()
     partners = [*near, *y_dev, *sq_dev, *z_dev[1:], x_dev]
+    weights_in = (
+        pltpu.make_async_copy(wu_hbm, wu, in_ss.at[0]),
+        pltpu.make_async_copy(wd_hbm, wd, in_ss.at[1]),
+    )
     for dev in partners:
         pl.semaphore_signal(barrier, inc=1, device_id=dev, device_id_type=MESH)
 
+    for copy in weights_in:
+        copy.start()
+
     def halo(d):
-        src = x_in.at[pl.ds(TOK - 16, 16)] if d == 0 else x_in.at[pl.ds(0, 16)]
-        return send(src, hin.at[d], halo_ss.at[d], halo_rs.at[d], sq_dev[d])
+        return send(h_st.at[d], hin.at[d], halo_ss.at[d], halo_rs.at[d], sq_dev[d])
 
     def weight(i):
         src, dst = ((wd, wd_p), (wu, wu_p), (wu_t, wu_tp))[i]
@@ -205,50 +211,51 @@
     def gk_z(j):
         return send(gk_m, gk_2.at[j], gk_ss.at[j], gk_rs.at[j], z_dev[j])
 
-    def core_w(i):
-        return send(c_s.at[i], c_r.at[i], c_ss.at[i], c_rs.at[i], near[1])
-
-    def ring(d, step, e):
-        i = (d * 4 + step) * 2 + e
-        if step == 0:
-            return send(
-                z_s.at[d, step, e, pl.ds(d, 1)], z_r.at[d, step, e, pl.ds(d, 1)],
-                z_ss.at[i], z_rs.at[i], z_ring[d],
-            )
-        return send(z_s.at[d, step, e], z_r.at[d, step, e], z_ss.at[i], z_rs.at[i], z_ring[d])
-
-    def x_swap():
+    def core_w(i, a):
+        j = i * 2 + a
+        return send(c_s.at[i, a], c_r.at[i, a], c_ss.at[j], c_rs.at[j], near[1])
+
+    def ring(d, step, p):
+        i = (d * 4 + step) * 3 + p
+        src, dst = z_s.at[d, step, p], z_r.at[d, step, p]
+        if step == 0 and p == 2:
+            half = pl.ds(d * (W // 2), W // 2)
+            src, dst = src.at[half], dst.at[half]
+        return send(src, dst, z_ss.at[i], z_rs.at[i], z_ring[d])
+
+    def x_early(i):
+        return send(e_s.at[i], e_r.at[i], e_ss.at[i], e_rs.at[i], x_dev)
+
+    def x_late():
         return send(x_s, x_r, x_ss.at[0], x_rs.at[0], x_dev)
 
     turn = lax.rem(D - tp * W, D)
-    scale_row = pltpu.roll(jnp.broadcast_to(scale[...], (8, D)), turn, 1)[0:1, 0:W]
-    gain_row = pltpu.roll(jnp.broadcast_to(gain[...], (8, D)), turn, 1)[0:1, 0:128]
-    cols[...] = jnp.broadcast_to(gain_row, (128, 128)).T
+
+    def local_column(ref):
+        row = pltpu.roll(jnp.broadcast_to(ref[...].reshape(1, D), (8, D)), turn, 1)[0:1, 0:128]
+        return jnp.broadcast_to(row, (128, 128)).T[0:W, 0:1]
+
+    scale_col = local_column(scale)
     for c in range(NC):
         for h in range(2):
-            rows = pl.ds(h * HALF + c * TC, TC)
-            s_st[h, c] = (scale_row * go[rows, :].astype(F32)).T.astype(BF)
-
+            at_ = pl.ds(h * HALF + c * TC, TC)
+            s_st[h, c] = (scale_col * go_t[:, at_].astype(F32)).astype(BF)
+    h_st[0] = x_t[:, pl.ds(TOK - 128, 128)].astype(F32).T[112:128].astype(BF)
+    h_st[1] = x_t[:, pl.ds(0, 128)].astype(F32).T[0:16].astype(BF)
+    cols[...] = jnp.broadcast_to(local_column(gain), (W, 128))
+
+    def load(i, carry):
+        block_t = x_t[:, pl.ds(pl.multiple_of(i * ROWS, ROWS), ROWS)].astype(F32)
+        xp[pl.ds(pl.multiple_of(EDGE + i * ROWS, 8), ROWS), :] = block_t.T
+        return carry
+
+    steps = TOK // ROWS
+    lax.fori_loop(0, steps, load, 0)
     pl.semaphore_wait(barrier, len(partners))
     for d in range(2):
         go_out(halo(d))
     for c in range(NC):
         gather_0(0, c)
-    for i in range(2):
-        go_out(weight(i))
-
-    def load(i, carry):
-        xp[pl.ds(pl.multiple_of(EDGE + i * ROWS, 8), ROWS), :] = x_in[
-            pl.ds(pl.multiple_of(i * ROWS, ROWS), ROWS), :
-        ].astype(F32)
-        return carry
-
-    lax.fori_loop(0, TOK // ROWS, load, 0)
-    for d in range(2):
-        halo(d).wait_recv()
-    xp[0:EDGE, :] = jnp.where(sq == 0, 0.0, hin[0].astype(F32)[8:16])
-    xp[pl.ds(EDGE + TOK, EDGE), :] = jnp.where(sq == SEQ - 1, 0.0, hin[1].astype(F32)[0:8])
-
     def conv_rows(i, carry):
         total = None
         for tap in range(KW):
@@ -261,16 +268,37 @@
         st_s[1:2, at_] = jnp.sum(out * out, axis=0, keepdims=True)
         return carry
 
-    lax.fori_loop(0, TOK // ROWS, conv_rows, 0)
+    lax.fori_loop(1, steps // 2, conv_rows, 0)
+    gather_1(0, 0)
+    for d in range(2):
+        halo(d).wait_recv()
+    xp[0:EDGE, :] = jnp.where(sq == 0, 0.0, hin[0].astype(F32)[8:16])
+    xp[pl.ds(EDGE + TOK, EDGE), :] = jnp.where(sq == SEQ - 1, 0.0, hin[1].astype(F32)[0:8])
+    gather_1(0, 1)
+    conv_rows(0, 0)
+    lax.fori_loop(steps // 2, steps, conv_rows, 0)
     for j in range(3):
         go_out(stat(0, j))
-    gather_1(0, 0)
+    gather_1(0, 2)
+    gather_2(0, 0)
+    gather_1(0, 3)
     for j in range(3):
         stat(0, j).wait_recv()
     st_m[...] = (st_s[...] + st_1[1]) + (st_1[0] + st_1[2])
     for j in range(3):
         go_out(stat(1, j))
-    gather_1(0, 1)
+    for copy in weights_in:
+        copy.wait()
+    for i in range(2):
+        go_out(weight(i))
+    gather_3(0, 0)
+
+    for i in range(D // 128):
+        part = slice(i * 128, (i + 1) * 128)
+        wu_t[:, part] = wu[part, :].T
+        gb[part, :] = jnp.broadcast_to(gain[part].reshape(1, 128), (128, 128)).T
+    go_out(weight(2))
+
     for j in range(3):
         stat(1, j).wait_recv()
     totals = (st_m[...] + st_2[2]) + (st_2[0] + st_2[1])
@@ -278,39 +306,27 @@
     var = totals[1:2] / D - mean * mean
     mr[0:1, :] = mean
     mr[1:2, :] = lax.rsqrt(var + 1e-06)
-    gain_col = cols[0:W, 0:1]
+    gain_col = cols[:, 0:1]
     for c in range(NC):
         for h in range(2):
             at_ = pl.ds(h * HALF + c * TC, TC)
             nhat = (cv[:, at_] - mr[0:1, at_]) * mr[1:2, at_]
             n_st[h, c] = (nhat * gain_col).astype(BF)
         gather_0(1, c)
-
-    for c in range(2, NC):
-        gather_1(0, c)
-
-    for i in range(D // 128):
-        part = slice(i * 128, (i + 1) * 128)
-        wu_t[:, part] = wu[part, :].T
-        gb[part, :] = jnp.broadcast_to(gain[0:1, part], (128, 128)).T
-    go_out(weight(2))
-
-    gather_2(0, 0)
+    gather_2(0, 1)
     gather_1(1, 0)
-    gather_2(0, 1)
+    gather_2(0, 2)
+    gather_3(0, 1)
     gather_1(1, 1)
-    gather_3(0, 0)
-    gather_2(0, 2)
-    gather_1(1, 2)
     gather_2(0, 3)
-    gather_1(1, 3)
+    gather_3(0, 2)
     for i in range(3):
         weight(i).wait_recv()
 
     def cotangent(c):
         gather_end(0, c)
-        gh_s[c, 0:U] = nn(wd[...], g_s[c])
-        gh_s[c, U:] = nn(wd_p[...], g_s[c])
+        pf[c, 0:U] = nn(wd[...], g_s[c])
+        pf[c, U : 2 * U] = nn(wd_p[...], g_s[c])
 
     def rs2_step(c):
         for d, to in ((0, up), (1, down)):
@@ -335,24 +351,23 @@
             go_out(rs3(c, j))
         own[c] = group(xh * 2 + k)
 
-    def layers(c):
+    def layers(c, u):
         at_ = pl.ds(c * TC, TC)
-        acc = jnp.zeros((8, TC), F32)
-        for u, w_t in enumerate((wu_t, wu_tp)):
-            pre_s[...] = nn(w_t[...], g_n[c])
-
-            def act(i, acc, u=u):
-                v = pre_s[rows_at(i * 32, 32), :]
-                to = rows_at(u * U + i * 32, 32)
-                phi = 0.5 + 0.5 * lax.erf(v * 0.7071067811865476)
-                slope = phi + v * jnp.exp(-0.5 * v * v) * 0.3989422804014327
-                gp = (gh_s[c, to] * slope).astype(BF)
-                hid[to, at_] = (v * phi).astype(BF)
-                gpr[to, at_] = gp
-                return acc + jnp.sum((gp.astype(F32) * v).reshape(4, 8, TC), axis=0)
-
-            acc = lax.fori_loop(0, U // 32, act, acc)
-        bst[1:2, at_] = jnp.sum(acc, axis=0, keepdims=True)
+        pre_s[...] = nn((wu_t, wu_tp)[u][...], g_n[c])
+
+        def act(i, acc):
+            v = pre_s[rows_at(i * 32, 32), :]
+            to = rows_at(u * U + i * 32, 32)
+            phi = 0.5 + 0.5 * lax.erf(v * 0.7071067811865476)
+            slope = phi + v * jnp.exp(-0.5 * v * v) * 0.3989422804014327
+            gp = (pf[c, to] * slope).astype(BF)
+            hid[to, at_] = (v * phi).astype(BF)
+            gpr[to, at_] = gp
+            return acc + jnp.sum((gp.astype(F32) * v).reshape(4, 8, TC), axis=0)
+
+        acc = lax.fori_loop(0, U // 32, act, jnp.zeros((8, TC), F32))
+        total = jnp.sum(acc, axis=0, keepdims=True)
+        bst[1:2, at_] = total if u == 0 else bst[1:2, at_] + total
 
     def back(c):
         at_ = pl.ds(c * TC, TC)
@@ -373,115 +388,158 @@
     cotangent(0)
     cotangent(1)
     gather_2(1, 0)
+    gather_1(1, 2)
+    gather_3(0, 3)
     cotangent(2)
     gather_2(1, 1)
     gather_3(1, 0)
+    gather_1(1, 3)
     cotangent(3)
+    gather_3(1, 1)
     gather_end(1, 0)
-    layers(0)
-    gather_3(1, 1)
+    layers(0, 0)
     gather_2(1, 2)
+    layers(0, 1)
+    gather_3(1, 2)
     back(0)
+    gather_end(1, 1)
+    layers(1, 0)
     gather_2(1, 3)
-    gather_end(1, 1)
-    layers(1)
-    gather_3(1, 2)
+    layers(1, 1)
+    gather_3(1, 3)
     back(1)
     rs2_step(0)
-    gather_3(1, 3)
     gather_end(1, 2)
-    layers(2)
-    rs3_step(0)
+    layers(2, 0)
+    layers(2, 1)
     back(2)
     rs2_step(1)
     gather_end(1, 3)
-    layers(3)
-    back(3)
-    for j in range(3):
-        go_out(bstat(0, j))
+    layers(3, 0)
+    rs3_step(0)
+    layers(3, 1)
 
     order = (4, 3, 5, 2, 6, 1, 7, 0)
 
+    def place(i):
+        return lax.rem(z + order[i], NZ)
+
     def weight_blocks(first, count):
-        for a, (left, right) in enumerate(((g_n, gpr), (g_s, hid))):
+        for a, left, right in ((1, g_s, hid), (0, g_n, gpr)):
             wide = []
             for c in range(NC):
                 pieces = []
-                for i in range(count):
-                    b = lax.rem(z + order_at(first, i), NZ)
+                for i in range(first, first + count):
                     for e in range(2):
-                        pieces.append(left[c, rows_at(e * (NZ * W) + b * W, W), :])
+                        pieces.append(left[c, rows_at(e * (NZ * W) + place(i) * W, W), :])
                 wide.append(jnp.concatenate(pieces, axis=0))
             lhs = jnp.concatenate(wide, axis=1)
             theirs = nt(lhs, right[U:, :])
+            for j in range(2 * count):
+                c_s[first + j // 2, a, j % 2] = theirs[j * W : (j + 1) * W].astype(BF)
+            for i in range(first, first + count):
+                go_out(core_w(i, a))
             mine = nt(lhs, right[0:U, :])
-            for i in range(count):
-                b = lax.rem(z + order_at(first, i), NZ)
-                for e in range(2):
-                    part = slice((i * 2 + e) * W, (i * 2 + e + 1) * W)
-                    c_s[first + i, e, a] = theirs[part].astype(BF)
-                    wf[b, e, a] = mine[part]
-        for i in range(count):
-            core_w(first + i).start()
-
-    def order_at(first, i):
-        return order[first + i]
-
-    def ring_step(i):
+            for j in range(2 * count):
+                wf[first + j // 2, a, j % 2] = mine[j * W : (j + 1) * W]
+
+    def both_cores(i, a, e):
+        return wf[i, a, e] + c_r[i, a, e].astype(F32)
+
+    def over_x(i):
+        core_w(i, 1).wait_recv()
+        e_s[i] = both_cores(i, 1, 1 - xl).astype(BF)
+        go_out(x_early(i))
+
+    def way(i):
         off = order[i]
-        b = lax.rem(z + off, NZ)
-        core_w(i).wait_recv()
-        if off == 4:
-            for e in range(2):
-                for d in range(2):
-                    got = wf[b, e, d] + c_r[i, e, d].astype(F32)
-                    z_s[d, 0, e, d] = got.astype(BF)
-                    go_out(ring(d, 0, e))
-        elif off != 0:
-            d = 0 if off < 4 else 1
-            step = 4 - off if off < 4 else off - 4
-            for e in range(2):
-                ring(d, step - 1, e).wait_recv()
-                for a in range(2):
-                    got = wf[b, e, a] + c_r[i, e, a].astype(F32)
-                    if step > 1 or a == d:
-                        got = got + z_r[d, step - 1, e, a].astype(F32)
-                    z_s[d, step, e, a] = got.astype(BF)
+        return (0, 4 - off) if off < 4 else (1, off - 4)
+
+    def ring_up(i):
+        core_w(i, 0).wait_recv()
+        if order[i] == 4:
+            for d in range(2):
+                z_s[d, 0, d] = both_cores(i, 0, d).astype(BF)
+                go_out(ring(d, 0, d))
+        elif order[i] != 0:
+            d, step = way(i)
+            for e in (d, 1 - d):
+                got = both_cores(i, 0, e)
+                if step > 1 or e == d:
+                    ring(d, step - 1, e).wait_recv()
+                    got = got + z_r[d, step - 1, e].astype(F32)
+                z_s[d, step, e] = got.astype(BF)
                 go_out(ring(d, step, e))
         else:
             for e in range(2):
                 for d in range(2):
                     ring(d, 3, e).wait_recv()
 
-            def part(e, a):
-                got = wf[b, e, a] + c_r[i, e, a].astype(F32)
-                return got + z_r[0, 3, e, a].astype(F32) + z_r[1, 3, e, a].astype(F32)
-
-            for a in range(2):
-                x_s[a] = part(1 - xl, a).astype(BF)
-            go_out(x_swap())
-            for a in range(2):
-                wf[b, xl, a] = part(xl, a)
-
+            def part(e):
+                return both_cores(i, 0, e) + z_r[0, 3, e].astype(F32) + z_r[1, 3, e].astype(F32)
+
+            x_s[...] = part(1 - xl).astype(BF)
+            go_out(x_late())
+            gu[...] = part(xl)
+
+    def ring_down(i):
+        x_early(i).wait_recv()
+        mine = both_cores(i, 1, xl) + e_r[i].astype(F32)
+        halves = (slice(0, W // 2), slice(W // 2, W))
+        if order[i] == 4:
+            for d, half in enumerate(halves):
+                z_s[d, 0, 2, half] = mine[half].astype(BF)
+                go_out(ring(d, 0, 2))
+        elif order[i] != 0:
+            d, step = way(i)
+            ring(d, step - 1, 2).wait_recv()
+            if step == 1:
+                half, rest = halves[d], halves[1 - d]
+                z_s[d, 1, 2, half] = (mine[half] + z_r[d, 0, 2, half].astype(F32)).astype(BF)
+                z_s[d, 1, 2, rest] = mine[rest].astype(BF)
+            else:
+                z_s[d, step, 2] = (mine + z_r[d, step - 1, 2].astype(F32)).astype(BF)
+            go_out(ring(d, step, 2))
+        else:
+            for d in range(2):
+                ring(d, 3, 2).wait_recv()
+            gd[...] = factor * (mine + z_r[0, 3, 2].astype(F32) + z_r[1, 3, 2].astype(F32))
+
+    factor = 1.0 / math.sqrt(TOK * SEQ)
     weight_blocks(0, 1)
-    rs3_step(1)
+    back(3)
+    for j in range(3):
+        go_out(bstat(0, j))
+    over_x(0)
+    ring_up(0)
     rs2_step(2)
     weight_blocks(1, 2)
-    ring_step(0)
+    ring_down(0)
+    over_x(1)
+    over_x(2)
     rs2_step(3)
-    rs3_step(2)
-    ring_step(1)
-    ring_step(2)
-    weight_blocks(3, 2)
+    ring_up(1)
+    ring_up(2)
+    rs3_step(1)
     for j in range(3):
         bstat(0, j).wait_recv()
     b_m[...] = (bst[...] + b_1[2]) + (b_1[0] + b_1[1])
     for j in range(3):
         go_out(bstat(1, j))
+    weight_blocks(3, 2)
+    ring_down(1)
+    ring_down(2)
+    over_x(3)
+    over_x(4)
+    rs3_step(2)
+    ring_up(3)
+    ring_up(4)
     rs3_step(3)
-    weight_blocks(5, 3)
-    ring_step(3)
-    ring_step(4)
+    weight_blocks(5, 2)
+    ring_down(3)
+    ring_down(4)
+    over_x(5)
+    over_x(6)
 
     for j in range(3):
         bstat(1, j).wait_recv()
@@ -504,6 +562,12 @@
             gc[pl.ds(EDGE + h * HALF + c * TC, TC), :] = grad.T
     for d in range(2):
         go_out(ghalo(d))
+    ring_up(5)
+    ring_up(6)
+    weight_blocks(7, 1)
+    ring_down(5)
+    ring_down(6)
+    over_x(7)
 
     def tap_rows(i, sums):
         g = gc[pl.ds(pl.multiple_of(EDGE + i * ROWS, 8), ROWS), :]
@@ -519,8 +583,8 @@
     gks[KW : KW + 1, :] = jnp.zeros((1, W), F32)
     go_out(gk_x())
 
-    ring_step(5)
-    ring_step(6)
+
+    ring_up(7)
 
     gk_x().wait_recv()
     gk_m[...] = gks[...] + gk_1[...]
@@ -533,30 +597,42 @@
 
     def back_rows(i, carry):
         at_ = pl.ds(pl.multiple_of(i * ROWS, ROWS), ROWS)
-        total = go[at_, :].astype(F32)
+        total = None
         for tap in range(KW):
-            total = total + taps[tap : tap + 1, :] * gc[pl.ds(i * ROWS + KW - tap, ROWS), :]
-        gi[at_, :] = total.astype(BF)
+            term = taps[tap : tap + 1, :] * gc[pl.ds(i * ROWS + KW - tap, ROWS), :]
+            total = term if total is None else total + term
+        gi_t[:, at_] = (go_t[:, at_].astype(F32) + total.T).astype(BF)
         return carry
 
     lax.fori_loop(0, TOK // ROWS, back_rows, 0)
 
-    factor = 1.0 / math.sqrt(TOK * SEQ)
     total = gk_m[...]
     for j in range(1, NZ):
         gk_z(j).wait_recv()
         total = total + gk_2[j]
     gk[...] = total[0:KW] * factor
 
-    ring_step(7)
-    x_swap().wait_recv()
-    gu[...] = (wf[z, xl, 0] + x_r[0].astype(F32)) * factor
-    gd[...] = (wf[z, xl, 1] + x_r[1].astype(F32)) * factor
+    ring_down(7)
+    x_late().wait_recv()
+    gu[...] = (gu[...] + x_r[...].astype(F32)) * factor
 
     for copy in sent:
         copy.wait_send()
-    for i in range(NZ):
-        core_w(i).wait_send()
+
+
+def hand_on(*arrays):
+    def copy_all(*refs):
+        n = len(arrays)
+        for src, dst in zip(refs[:n], refs[n:]):
+            dst[...] = src[...]
+
+    spec = pl.BlockSpec(memory_space=pltpu.VMEM)
+    return pl.pallas_call(
+        copy_all,
+        out_shape=[jax.ShapeDtypeStruct(a.shape, a.dtype) for a in arrays],
+        in_specs=[spec] * len(arrays),
+        out_specs=[spec] * len(arrays),
+    )(*arrays)
 
 
 def block(inputs, grad_out, kernel, ln_gain, layer_scale, w_up, w_down):
@@ -569,19 +645,21 @@
         vmem((TOK + 2 * EDGE, W), F32),
         vmem((W, TOK), F32),
         vmem((2, 16, W), BF),
+        vmem((2, 16, W), BF),
         vmem((2, TOK), F32),
         vmem((3, 2, TOK), F32),
         vmem((2, TOK), F32),
         vmem((3, 2, TOK), F32),
         vmem((2, TOK), F32),
-        vmem((128, 128), F32),
+        vmem((W, 128), F32),
         vmem((D, 128), F32),
+        vmem((D, U), BF),
+        vmem((U, D), BF),
         vmem((U, D), BF),
         vmem((D, U), BF),
         vmem((U, D), BF),
         vmem((U, D), BF),
         vmem((U, TC), F32),
-        vmem((NC, 2 * U, TC), F32),
         vmem((2 * U, HALF), BF),
         vmem((2 * U, HALF), BF),
         vmem((NC, D, TC), F32),
@@ -605,29 +683,33 @@
         vmem((NZ, 2, 2, W, U), F32),
         vmem((NZ, 2, 2, W, U), BF),
         vmem((NZ, 2, 2, W, U), BF),
-        vmem((2, 4, 2, 2, W, U), BF),
-        vmem((2, 4, 2, 2, W, U), BF),
-        vmem((2, W, U), BF),
-        vmem((2, W, U), BF),
+        vmem((2, 4, 3, W, U), BF),
+        vmem((2, 4, 3, W, U), BF),
+        vmem((W, U), BF),
+        vmem((W, U), BF),
+        vmem((NZ, W, U), BF),
+        vmem((NZ, W, U), BF),
     ]
-    for count in (2, 3, 6, 24 * NC, 2 * NC, 2 * NC, 3 * NC, 6, 2, NZ, NZ, 16, 1):
+    for count in (2, 3, 6, 24 * NC, 2 * NC, 2 * NC, 3 * NC, 6, 2, NZ, 2 * NZ, 24, 1, NZ, 2):
         scratch += [dma((count,)), dma((count,))]
     spec = pl.BlockSpec(memory_space=pltpu.VMEM)
-    return pl.pallas_call(
+    gi_t, gu, gd, gk = pl.pallas_call(
         body,
         out_shape=[
-            jax.ShapeDtypeStruct((TOK, W), BF),
+            jax.ShapeDtypeStruct((W, TOK), BF),
             jax.ShapeDtypeStruct((W, U), F32),
             jax.ShapeDtypeStruct((W, U), F32),
             jax.ShapeDtypeStruct((KW, W), F32),
         ],
-        in_specs=[spec] * 7,
+        in_specs=[spec] * 5 + [pl.BlockSpec(memory_space=pl.ANY)] * 2,
         out_specs=[spec] * 4,
         scratch_shapes=scratch,
         compiler_params=pltpu.CompilerParams(
             collective_id=0, has_side_effects=True, vmem_limit_bytes=60 * 2**20
         ),
-    )(inputs, grad_out, kernel, ln_gain[None, :], layer_scale[None, :], w_up, w_down)
+    )(inputs.T, grad_out.T, kernel, ln_gain, layer_scale, w_up, w_down)
+    gi_t, gu, gd, gk = hand_on(gi_t, gu, gd, gk)
+    return gi_t.T, gu, gd, gk
 
 
 def solution(mesh):

time: 136 us -> 114 us (0.84)
  Pallas kernels: 124 us -> 113 us
  local copies, waits for them, and re-layouts: 10.5 us -> 0 us
    pallas_call x1 -> x2, Pallas kernels: 124 us -> 113 us  [the longest x1 111 us: block(): pl.pallas_call(body, out_shape=[jax.ShapeDtypeStruct((W, TOK), BF), jax.S...]
    unnamed x11 -> x0, local copies, waits for them, and re-layouts: 5.84 us -> none
    broadcast_in_dim x2 -> x0, local copies, waits for them, and re-layouts: 2.64 us -> none  [the longest x1 1.34 us: block(): ln_gain[None, :]]
    pallas_call x1 -> x0, local copies, waits for them, and re-layouts: 2.02 us -> none  [block(): pl.pallas_call(body, out_shape=[jax.ShapeDtypeStruct((TOK, W), BF), jax.S...]
where the time goes in v3:
time: 114 us
  Pallas kernels  113 us (99%)
    pallas_call x1, Pallas kernels, block(): pl.pallas_call(body, out_shape=[jax.ShapeDtypeStruct((W, TOK), BF), jax.S...  111 us

profile of v3, /device:TPU:2, one launch (start us, length us, event | category | flops | bytes accessed | tf_op | source)
XLA Modules:
  0.0 113.7 jit_solution(2688873280110897964)
XLA Ops:
  0.6 111.1 %shard_map.102 = (bf16[96,2048]{1,0:T(8,128)(2,1)}, f32[96,384]{1,0:T(8,128)}, f32[96,384]{1,0:T(8,128)}, f32[15,96]{1,0:T(8,128)}) custom-call(bf16[96,2048]{1,0:T(8,128)(2,1)} %bitcast.3, bf16[96,2048]{1,0:T(8,128)(2,1)} %bitcast.4, f32[15,96]{1,0:T(8,128)} %taps.1, f32[1536]{0:T(1024)} %gain.1, f32[1536]{0:T(1024)} %scale.1, bf16[1536,384]{1,0:T(8,128)(2,1)} %wu_hbm.1, ...), custom_call_target="tpu_custom_call" | custom-call | tf_op jit(solution)/shard_map/pallas_call | solution.py:696
  111.7 2.0 %shard_map.103 = (bf16[96,2048]{1,0:T(8,128)(2,1)}, f32[96,384]{1,0:T(8,128)}, f32[96,384]{1,0:T(8,128)}, f32[15,96]{1,0:T(8,128)}) custom-call(bf16[96,2048]{1,0:T(8,128)(2,1)} %get-tuple-element.12.refs_0_, f32[96,384]{1,0:T(8,128)} %get-tuple-element.13.refs_1_, f32[96,384]{1,0:T(8,128)} %get-tuple-element.14.refs_2_, f32[15,96]{1,0:T(8,128)} %get-tuple-element.15.refs_3_), custom_call_target="tpu_custom_call" | custom-call | tf_op jit(solution)/shard_map/pallas_call | solution.py:630

commit v4 on v3

--- a/solution.py
+++ b/solution.py
@@ -26,7 +26,7 @@
 EDGE = 8
 ROWS = 128
 
-X_FIRST = ((False, True, False, True), (True, False, True, True))
+X_FIRST = ((False, True, False, True), (False, True, True, True))
 
 
 def nn(a, b):
@@ -424,8 +424,9 @@
     def place(i):
         return lax.rem(z + order[i], NZ)
 
-    def weight_blocks(first, count):
-        for a, left, right in ((1, g_s, hid), (0, g_n, gpr)):
+    def weight_blocks(first, count, which=(1, 0)):
+        for a in which:
+            left, right = ((g_n, gpr), (g_s, hid))[a]
             wide = []
             for c in range(NC):
                 pieces = []
@@ -506,12 +507,12 @@
             gd[...] = factor * (mine + z_r[0, 3, 2].astype(F32) + z_r[1, 3, 2].astype(F32))
 
     factor = 1.0 / math.sqrt(TOK * SEQ)
-    weight_blocks(0, 1)
+    weight_blocks(0, 1, (0, 1))
+    ring_up(0)
+    over_x(0)
     back(3)
     for j in range(3):
         go_out(bstat(0, j))
-    over_x(0)
-    ring_up(0)
     rs2_step(2)
     weight_blocks(1, 2)
     ring_down(0)
@@ -541,33 +542,22 @@
     over_x(5)
     over_x(6)
 
-    for j in range(3):
-        bstat(1, j).wait_recv()
-    for c in range(NC):
+    def norm_back(c):
+        rel = pl.ds(c * TC, TC)
         for j in range(3):
             rs3(c, j).wait_recv()
-    sums_here = (b_m[...] + b_2[0]) / D
-    sums_there = (b_2[1] + b_2[2]) / D
-    for h in range(2):
-        sums = jnp.where(k == h, sums_here, sums_there)
-        for c in range(NC):
+        here = own[c] + r3[c, 0].astype(F32)
+        there = r3[c, 1].astype(F32) + r3[c, 2].astype(F32)
+        sums_here = (b_m[:, rel] + b_2[0, :, rel]) / D
+        sums_there = (b_2[1, :, rel] + b_2[2, :, rel]) / D
+        for h in range(2):
             at_ = pl.ds(h * HALF + c * TC, TC)
-            rel = slice(c * TC, (c + 1) * TC)
-            here = own[c] + r3[c, 0].astype(F32)
-            there = r3[c, 1].astype(F32) + r3[c, 2].astype(F32)
+            sums = jnp.where(k == h, sums_here, sums_there)
             scaled_g = jnp.where(k == h, here, there) * gain_col
             rstd = mr[1:2, at_]
             nhat = (cv[:, at_] - mr[0:1, at_]) * rstd
-            grad = rstd * (scaled_g - sums[0:1, rel] - nhat * sums[1:2, rel])
+            grad = rstd * (scaled_g - sums[0:1] - nhat * sums[1:2])
             gc[pl.ds(EDGE + h * HALF + c * TC, TC), :] = grad.T
-    for d in range(2):
-        go_out(ghalo(d))
-    ring_up(5)
-    ring_up(6)
-    weight_blocks(7, 1)
-    ring_down(5)
-    ring_down(6)
-    over_x(7)
 
     def tap_rows(i, sums):
         g = gc[pl.ds(pl.multiple_of(EDGE + i * ROWS, 8), ROWS), :]
@@ -576,24 +566,6 @@
             prod = g * xp[pl.ds(i * ROWS + tap + 1, ROWS), :]
             out.append(sums[tap] + jnp.sum(prod.reshape(ROWS // 8, 8, W), axis=0))
         return tuple(out)
-
-    sums = lax.fori_loop(0, TOK // ROWS, tap_rows, (jnp.zeros((8, W), F32),) * KW)
-    for tap in range(KW):
-        gks[tap : tap + 1, :] = jnp.sum(sums[tap], axis=0, keepdims=True)
-    gks[KW : KW + 1, :] = jnp.zeros((1, W), F32)
-    go_out(gk_x())
-
-
-    ring_up(7)
-
-    gk_x().wait_recv()
-    gk_m[...] = gks[...] + gk_1[...]
-    for j in range(1, NZ):
-        go_out(gk_z(j))
-    for d in range(2):
-        ghalo(d).wait_recv()
-    gc[0:EDGE, :] = jnp.where(sq == 0, 0.0, gch[0])
-    gc[pl.ds(EDGE + TOK, EDGE), :] = jnp.where(sq == SEQ - 1, 0.0, gch[1])
 
     def back_rows(i, carry):
         at_ = pl.ds(pl.multiple_of(i * ROWS, ROWS), ROWS)
@@ -604,14 +576,46 @@
         gi_t[:, at_] = (go_t[:, at_].astype(F32) + total.T).astype(BF)
         return carry
 
-    lax.fori_loop(0, TOK // ROWS, back_rows, 0)
-
+    for j in range(3):
+        bstat(1, j).wait_recv()
+    for c in range(NC - 1):
+        norm_back(c)
+    half_steps, early = steps // 2, (NC - 1) * TC // ROWS
+    sums = (jnp.zeros((8, W), F32),) * KW
+    for h in range(2):
+        sums = lax.fori_loop(h * half_steps, h * half_steps + early, tap_rows, sums)
+    norm_back(NC - 1)
+    for d in range(2):
+        go_out(ghalo(d))
+    for h in range(2):
+        sums = lax.fori_loop(h * half_steps + early, (h + 1) * half_steps, tap_rows, sums)
+    for tap in range(KW):
+        gks[tap : tap + 1, :] = jnp.sum(sums[tap], axis=0, keepdims=True)
+    gks[KW : KW + 1, :] = jnp.zeros((1, W), F32)
+    go_out(gk_x())
+    ring_up(5)
+    ring_up(6)
+    weight_blocks(7, 1)
+    ring_down(5)
+    ring_down(6)
+    gk_x().wait_recv()
+    gk_m[...] = gks[...] + gk_1[...]
+    for j in range(1, NZ):
+        go_out(gk_z(j))
+    over_x(7)
+    lax.fori_loop(1, steps - 1, back_rows, 0)
+    ring_up(7)
+    for d in range(2):
+        ghalo(d).wait_recv()
+    gc[0:EDGE, :] = jnp.where(sq == 0, 0.0, gch[0])
+    gc[pl.ds(EDGE + TOK, EDGE), :] = jnp.where(sq == SEQ - 1, 0.0, gch[1])
+    back_rows(0, 0)
+    back_rows(steps - 1, 0)
     total = gk_m[...]
     for j in range(1, NZ):
         gk_z(j).wait_recv()
         total = total + gk_2[j]
     gk[...] = total[0:KW] * factor
-
     ring_down(7)
     x_late().wait_recv()
     gu[...] = (gu[...] + x_r[...].astype(F32)) * factor

time: 114 us -> 110 us (0.965)
  Pallas kernels: 113 us -> 109 us
    pallas_call x1, Pallas kernels: 111 us -> 107 us  [block(): pl.pallas_call(body, out_shape=[jax.ShapeDtypeStruct((W, TOK), BF), jax.S...]
where the time goes in v4:
time: 110 us
  Pallas kernels  109 us (99%)
    pallas_call x1, Pallas kernels, block(): pl.pallas_call(body, out_shape=[jax.ShapeDtypeStruct((W, TOK), BF), jax.S...  107 us

profile of v4, /device:TPU:2, one launch (start us, length us, event | category | flops | bytes accessed | tf_op | source)
XLA Modules:
  0.0 109.9 jit_solution(4046512794827348453)
XLA Ops:
  0.6 107.3 %shard_map.102 = (bf16[96,2048]{1,0:T(8,128)(2,1)}, f32[96,384]{1,0:T(8,128)}, f32[96,384]{1,0:T(8,128)}, f32[15,96]{1,0:T(8,128)}) custom-call(bf16[96,2048]{1,0:T(8,128)(2,1)} %bitcast.3, bf16[96,2048]{1,0:T(8,128)(2,1)} %bitcast.4, f32[15,96]{1,0:T(8,128)} %taps.1, f32[1536]{0:T(1024)} %gain.1, f32[1536]{0:T(1024)} %scale.1, bf16[1536,384]{1,0:T(8,128)(2,1)} %wu_hbm.1, ...), custom_call_target="tpu_custom_call" | custom-call | tf_op jit(solution)/shard_map/pallas_call | solution.py:700
  107.9 2.0 %shard_map.103 = (bf16[96,2048]{1,0:T(8,128)(2,1)}, f32[96,384]{1,0:T(8,128)}, f32[96,384]{1,0:T(8,128)}, f32[15,96]{1,0:T(8,128)}) custom-call(bf16[96,2048]{1,0:T(8,128)(2,1)} %get-tuple-element.12.refs_0_, f32[96,384]{1,0:T(8,128)} %get-tuple-element.13.refs_1_, f32[96,384]{1,0:T(8,128)} %get-tuple-element.14.refs_2_, f32[15,96]{1,0:T(8,128)} %get-tuple-element.15.refs_3_), custom_call_target="tpu_custom_call" | custom-call | tf_op jit(solution)/shard_map/pallas_call | solution.py:634

commit v5 on v4

--- a/solution.py
+++ b/solution.py
@@ -413,8 +413,8 @@
     layers(2, 0)
     layers(2, 1)
     back(2)
+    gather_end(1, 3)
     rs2_step(1)
-    gather_end(1, 3)
     layers(3, 0)
     rs3_step(0)
     layers(3, 1)
@@ -625,17 +625,28 @@
 
 
 def hand_on(*arrays):
+    n = len(arrays)
+
     def copy_all(*refs):
-        n = len(arrays)
-        for src, dst in zip(refs[:n], refs[n:]):
-            dst[...] = src[...]
-
-    spec = pl.BlockSpec(memory_space=pltpu.VMEM)
+        srcs, dsts, held, sem = refs[:n], refs[n : 2 * n], refs[2 * n : 3 * n], refs[3 * n]
+        into = [pltpu.make_async_copy(srcs[i], held[i], sem.at[i]) for i in range(n)]
+        out = [pltpu.make_async_copy(held[i], dsts[i], sem.at[n + i]) for i in range(n)]
+        for copy in into:
+            copy.start()
+        for i in range(n):
+            into[i].wait()
+            out[i].start()
+        for copy in out:
+            copy.wait()
+
+    spec = pl.BlockSpec(memory_space=pl.ANY)
     return pl.pallas_call(
         copy_all,
         out_shape=[jax.ShapeDtypeStruct(a.shape, a.dtype) for a in arrays],
-        in_specs=[spec] * len(arrays),
-        out_specs=[spec] * len(arrays),
+        in_specs=[spec] * n,
+        out_specs=[spec] * n,
+        scratch_shapes=[pltpu.VMEM(a.shape, a.dtype) for a in arrays]
+        + [pltpu.SemaphoreType.DMA((2 * n,))],
     )(*arrays)
 
 

time: 110 us -> 110 us (level)
  no operation moved by 1% of the time
where the time goes in v5:
time: 110 us
  Pallas kernels  109 us (99%)
    pallas_call x1, Pallas kernels, block(): pl.pallas_call(body, out_shape=[jax.ShapeDtypeStruct((W, TOK), BF), jax.S...  107 us

profile of v5, /device:TPU:2, one launch (start us, length us, event | category | flops | bytes accessed | tf_op | source)
XLA Modules:
  0.0 110.0 jit_solution(3563638408521226953)
XLA Ops:
  0.6 107.3 %shard_map.102 = (bf16[96,2048]{1,0:T(8,128)(2,1)}, f32[96,384]{1,0:T(8,128)}, f32[96,384]{1,0:T(8,128)}, f32[15,96]{1,0:T(8,128)}) custom-call(bf16[96,2048]{1,0:T(8,128)(2,1)} %bitcast.3, bf16[96,2048]{1,0:T(8,128)(2,1)} %bitcast.4, f32[15,96]{1,0:T(8,128)} %taps.1, f32[1536]{0:T(1024)} %gain.1, f32[1536]{0:T(1024)} %scale.1, bf16[1536,384]{1,0:T(8,128)(2,1)} %wu_hbm.1, ...), custom_call_target="tpu_custom_call" | custom-call | tf_op jit(solution)/shard_map/pallas_call | solution.py:711
  107.9 1.9 %shard_map.103 = (bf16[96,2048]{1,0:T(8,128)(2,1)}, f32[96,384]{1,0:T(8,128)}, f32[96,384]{1,0:T(8,128)}, f32[15,96]{1,0:T(8,128)}) custom-call(bf16[96,2048]{1,0:T(8,128)(2,1)} %get-tuple-element.12.refs_0_, f32[96,384]{1,0:T(8,128)} %get-tuple-element.13.refs_1_, f32[96,384]{1,0:T(8,128)} %get-tuple-element.14.refs_2_, f32[15,96]{1,0:T(8,128)} %get-tuple-element.15.refs_3_), custom_call_target="tpu_custom_call" | custom-call | tf_op jit(solution)/shard_map/pallas_call | solution.py:643
